TPU v7x, 256 devices: a whole 4x4x8 slice. The times are simulated.
256 devices in a mesh: row: 32 (over z_lo, y, core), col: 8 (over z_hi, x).
Axes of the slice: x: 4, y: 4, z: 8 (z_hi: 2, z_lo: 4; z = z_hi * 4 + z_lo), core: 2. Of those that a mesh axis runs over, the one named last changes fastest.
Arguments:
- damping: bfloat16 [1536, 128, 1536], P('col', 'row'), may hold values from -60 to 60
- block_seeds: int32 [32], replicated, may hold values from 1 to 65520
Outputs:
- basis: float32 [32, 1536, 32], P('row', 'col')
All inputs are finite; a program needn't handle non-finite values.
Results may differ from a plain program's by a relative error of at most 0.0057.
Values may be sent and summed in bfloat16 or wider, within the bound.
A program may use at most 64 MiB of HBM per device.

v0:
```python
import math

import jax
import jax.numpy as jnp
from jax import lax
from jax.sharding import PartitionSpec as P

NF = 128
M = 1536
P_SIZE = 32
NB = 32
NSTEPS = 12


def lag_table():
    lag_idx = jnp.arange(2 * NB, dtype=jnp.float32)[:, None]
    freq_idx = jnp.arange(NF, dtype=jnp.float32)[None, :]
    window = jnp.exp(-math.log(3.0) * lag_idx / NB)
    cos_table = (
        jnp.cos(math.pi * (freq_idx + 0.5) * lag_idx / NF)
        * window
        * math.sqrt(2.0 / NF)
        / math.sqrt(NB * M)
    )
    return cos_table.astype(jnp.bfloat16)


def probe_blocks(block_seeds, start_col, number):
    prime_mod = 65521
    column = (start_col + jnp.arange(number, dtype=jnp.int32))[None, :, None]
    probe_col = jnp.arange(P_SIZE, dtype=jnp.int32)[None, None, :]
    seed_col = block_seeds[:, None, None]
    inner_part = seed_col * (column + 1) % prime_mod * (column + 3) % prime_mod
    phase_val = (
        inner_part * (probe_col + 1) + seed_col * (probe_col + 1) % prime_mod * (probe_col + 2)
    ) % prime_mod
    return jnp.cos(2.0 * math.pi * phase_val.astype(jnp.float32) / prime_mod).astype(jnp.bfloat16)


def hankel_stack(blocks, group_len):
    extent = blocks.shape[0] + group_len - 1
    padded = jnp.pad(blocks, ((group_len - 1, group_len - 1), (0, 0), (0, 0)))
    shifted = [
        padded[group_len - 1 - offset : group_len - 1 - offset + extent]
        for offset in range(group_len)
    ]
    return jnp.stack(shifted, axis=2).reshape(extent, blocks.shape[1], group_len * blocks.shape[2])


def hankel_pass(lag_tiles, stack, shift_by, form, group_len):
    extent = stack.shape[0]
    pieces = []
    for group in range(NB // group_len):
        start_lag = group * group_len + shift_by
        window_lags = lag_tiles[start_lag : start_lag + extent]
        product = jnp.einsum(form, window_lags, stack, preferred_element_type=jnp.float32)
        pieces.append(product.reshape(product.shape[0], group_len, P_SIZE).transpose(1, 0, 2))
    return jnp.concatenate(pieces, axis=0)


def gram_of(blocks):
    return jnp.einsum("bcp,bcq->pq", blocks, blocks, precision=lax.Precision.HIGHEST)


def finish(mine, gram):
    highest = lax.Precision.HIGHEST
    scale = jnp.trace(gram) + 1e-06
    current = gram / scale
    eye_mat = jnp.eye(P_SIZE, dtype=jnp.float32)
    inverse = eye_mat
    for repeat in range(NSTEPS):
        weight = 1.5 * eye_mat - 0.5 * jnp.dot(inverse, current, precision=highest)
        current = jnp.dot(current, weight, precision=highest)
        inverse = jnp.dot(weight, inverse, precision=highest)
    factor = math.sqrt(NB * M) / jnp.sqrt(scale)
    return factor * jnp.einsum("bcp,pq->bcq", mine, inverse, precision=highest)


def shards(damping, block_seeds):
    group_len = min(16, NB)
    row_count = lax.axis_size("row")
    tile_cols = damping.shape[0]
    cos_table = lag_table()
    lag_tiles = jnp.einsum(
        "lk,nkr->lrn",
        cos_table,
        lax.all_to_all(damping, "row", split_axis=2, concat_axis=1, tiled=True),
        preferred_element_type=jnp.float32,
    ).astype(jnp.bfloat16)
    local_probes = probe_blocks(block_seeds, lax.axis_index("col") * tile_cols, tile_cols)
    partial_rows = hankel_pass(
        lag_tiles, hankel_stack(local_probes, group_len), 0, "lrc,lcn->rn", group_len
    )
    forward_b = lax.psum(partial_rows, "col").astype(jnp.bfloat16)
    partial_cols = hankel_pass(
        lag_tiles, hankel_stack(forward_b, group_len), 1, "lrc,lrn->cn", group_len
    )
    own_blocks = NB // row_count
    full_cols = lax.psum(partial_cols, "row")
    gram = lax.psum(gram_of(full_cols), "col")
    mine = lax.dynamic_slice_in_dim(full_cols, lax.axis_index("row") * own_blocks, own_blocks, 0)
    return finish(mine, gram)


def solution(mesh):
    return jax.shard_map(
        shards,
        mesh=mesh,
        in_specs=(P("col", "row", None), P()),
        out_specs=P("row", "col", None),
        check_vma=False,
    )
```

profile of v0, /device:TPU:1, one launch (start us, length us, event | category | flops | bytes accessed | tf_op | source)
XLA Modules:
  0.0 580.5 jit_solution(5123182008981434734)
XLA Ops:
  6.5 7.2 %copy.35 = bf16[192,4,1536]{0,1,2:T(4,128)(2,1)} copy(bf16[192,4,1536]{2,1,0:T(4,128)(2,1)} %param.2) | data formatting | bytes 4718592 | tf_op args[0]
  13.8 10.2 %all-to-all-start = ((bf16[192,4,1536]{0,1,2:T(4,128)(2,1)}), bf16[192,4,1536]{0,1,2:T(4,128)(2,1)S(1)}, u32[]{:S(2)}, u32[]{:S(2)}) async-start(bf16[192,4,1536]{0,1,2:T(4,128)(2,1)} %copy.35), calls=%async_computation | async-start | bytes 6291456 | tf_op jit(solution)/shard_map/all_to_all | solution.py:87
  24.3 4.4 fusion.38
  28.7 1.0 fusion.43
  29.7 1.0 fusion.45
  30.8 1.0 fusion.47
  31.8 1.0 fusion.49
  32.8 1.0 fusion.51
  33.8 1.0 fusion.53
  34.8 1.0 fusion.55
  35.9 1.0 fusion.57
  36.9 1.0 fusion.59
  37.9 1.0 fusion.61
  38.9 1.0 fusion.63
  39.9 1.0 fusion.65
  40.9 1.1 fusion.67
  42.0 1.0 fusion.69
  43.0 1.1 fusion.71
  44.0 1.0 fusion.73
  45.1 49.5 %all-to-all-done = bf16[192,4,1536]{0,1,2:T(4,128)(2,1)S(1)} async-done(((bf16[192,4,1536]{0,1,2:T(4,128)(2,1)}), bf16[192,4,1536]{0,1,2:T(4,128)(2,1)S(1)}, u32[]{:S(2)}, u32[]{:S(2)}) %all-to-all-start) | async-done | bytes 2359328 | tf_op jit(solution)/shard_map/all_to_all | solution.py:87
  95.4 1.4 fusion.9
  97.0 6.4 %fusion.12 = f32[16,48,32]{1,2,0:T(8,128)S(1)} fusion(bf16[47,192,16,32]{1,3,2,0:T(8,128)(2,1)} %fusion.73, bf16[47,48,192]{2,0,1:T(8,128)(2,1)S(1)} %get-tuple-element.6), kind=kOutput, calls=%fused_computation.45 | convolution fusion | flops 443547648 | bytes 10205184 | tf_op jit(solution)/shard_map/lrc,lcn->rn/dot_general | solution.py:56
  103.4 6.4 %fusion.15 = f32[16,48,32]{1,2,0:T(8,128)S(1)} fusion(bf16[47,192,16,32]{1,3,2,0:T(8,128)(2,1)} %fusion.73, bf16[47,48,192]{2,0,1:T(8,128)(2,1)S(1)} %get-tuple-element.5), kind=kOutput, calls=%fused_computation.46 | convolution fusion | flops 443547648 | bytes 10205184 | tf_op jit(solution)/shard_map/lrc,lcn->rn/dot_general | solution.py:56
  109.9 52.7 %all-reduce.6 = bf16[32,48,32]{1,2,0:T(8,128)(2,1)S(1)} all-reduce(f32[32,48,32]{1,2,0:T(8,128)S(1)} %pad_maximum_fusion.1), channel_id=1, replica_groups=mesh['row'=32,'col'=8] {'col'}, use_global_device_ids=true, to_apply=%region_0.1 | all-reduce | flops 49152 | bytes 294912 | tf_op jit(solution)/shard_map/psum | solution.py:94
  162.6 0.8 fusion.75
  164.2 0.8 fusion.79
  165.0 0.8 fusion.81
  165.8 0.8 fusion.83
  166.6 0.8 fusion.85
  167.5 0.8 fusion.87
  168.3 0.8 fusion.89
  169.1 0.8 fusion.91
  169.9 0.8 fusion.93
  170.7 0.9 fusion.95
  171.6 0.8 fusion.97
  173.2 0.8 fusion.101
  174.0 0.8 fusion.103
  175.6 12.8 %copy.58 = bf16[47,48,16,32]{3,2,1,0:T(8,128)(2,1)} copy(bf16[47,48,16,32]{1,3,0,2:T(8,128)(2,1)} %fusion.105) | data formatting | bytes 4620288 | tf_op jit(solution)/shard_map/stack | solution.py:47
  188.4 13.1 %reshape.180 = bf16[47,48,512]{2,1,0:T(8,128)(2,1)} reshape(bf16[47,48,16,32]{3,2,1,0:T(8,128)(2,1)} %copy.58) | data formatting | bytes 4620288 | tf_op jit(solution)/shard_map/reshape | solution.py:47
  201.5 11.2 %dot_general.140 = bf16[16,32,47,48]{1,0,3,2:T(8,128)(2,1)} reshape(bf16[512,47,48]{0,2,1:T(8,128)(2,1)} %bitcast.309) | data formatting | bytes 4620288 | tf_op jit(solution)/shard_map/lrc,lrn->cn/dot_general | solution.py:56
  212.7 14.9 %copy.59 = bf16[16,32,47,48]{2,1,3,0:T(8,128)(2,1)} copy(bf16[16,32,47,48]{1,0,3,2:T(8,128)(2,1)} %dot_general.140) | data formatting | bytes 4620288 | tf_op jit(solution)/shard_map/lrc,lrn->cn/dot_general | solution.py:56
  227.6 4.8 convolution_bitcast_fusion.1
  232.4 2.3 convolution_bitcast_fusion
  234.7 1.1 pad_maximum_fusion
  235.8 282.9 %all-reduce.5.cloned.1.call-done = f32[32,192,32]{1,2,0:T(8,128)} async-done(((f32[32,192,32]{1,2,0:T(8,128)}), f32[32,192,32]{1,2,0:T(8,128)}) %all-reduce.5.cloned.1.call-update) | async-done | bytes 786448 | tf_op jit(solution)/shard_map/psum | solution.py:99
  518.8 2.5 convolution_bitcast_fusion.2
  521.3 44.0 %psum.23 = f32[32,32]{1,0:T(8,128)S(1)} all-reduce(f32[32,32]{1,0:T(8,128)S(1)} %convolution_bitcast_fusion.2), channel_id=1, replica_groups=mesh['row'=32,'col'=8] {'col'}, use_global_device_ids=true, to_apply=%region_2.3 | all-reduce | flops 1024 | bytes 8192 | tf_op jit(solution)/shard_map/psum | solution.py:100
  572.0 1.6 fusion.22
  (55 shorter events, 9.5 us)
Async XLA Ops:
  6.5 17.5 %copy-start.1 = (s32[32]{0:T(128)S(1)}, s32[32]{0:T(128)}, u32[]{:S(2)}) copy-start(s32[32]{0:T(128)} %param.3) | copy-start | bytes 388
  13.8 80.9 %all-to-all-start = ((bf16[192,4,1536]{0,1,2:T(4,128)(2,1)}), bf16[192,4,1536]{0,1,2:T(4,128)(2,1)S(1)}, u32[]{:S(2)}, u32[]{:S(2)}) async-start(bf16[192,4,1536]{0,1,2:T(4,128)(2,1)} %copy.35), calls=%async_computation | async-start | bytes 6291456 | tf_op jit(solution)/shard_map/all_to_all | solution.py:87
  24.0 494.8 %all-reduce.5.cloned.1.call-start = ((), (), s32[]{:S(2)}) async-start(), calls=%async_computation.1 | async-start | bytes 2097152 | tf_op jit(solution)/shard_map/psum | solution.py:99
  227.6 4.8 copy-start
Sparse Core Ops, SparseCore 0:
  236.0 282.7 all-reduce.4
where the time goes:
time: 589 us; the launch traced here: 580 us
  waiting for transfers between devices  332 us (56%)
  blocking collectives  96.7 us (16%)
  local copies, waits for them, and re-layouts  89.6 us (15%)
  matrix products  30.6 us (5%)
  between operations  14.4 us (2%)
  starting transfers between devices  10.2 us (2%)
  other arithmetic  6.42 us (1%)
    psum x1, waiting for transfers between devices, shards(): full_cols = lax.psum(partial_cols, 'row')  283 us
    psum x1, blocking collectives, shards(): forward_b = lax.psum(partial_rows, 'col').astype(jnp.bfloat16)  52.7 us
    all_to_all x1, waiting for transfers between devices, shards(): lax.all_to_all(damping, 'row', split_axis=2, concat_axis=1, tiled=True)  49.5 us
    psum x1, blocking collectives, shards(): gram = lax.psum(gram_of(full_cols), 'col')  44 us
    unnamed x35, local copies, waits for them, and re-layouts  34.8 us
    dot_general x2, local copies, waits for them, and re-layouts, hankel_pass(): jnp.einsum(form, window_lags, stack, preferred_element_type=jnp.float32)  26.1 us
    dot_general x4, matrix products, hankel_pass(): jnp.einsum(form, window_lags, stack, preferred_element_type=jnp.float32)  19.9 us
    another operation x3, local copies, waits for them, and re-layouts, hankel_stack(): jnp.stack(shifted, axis=2)  14.6 us
  transfers between devices with their start and end apart: 2, of which 2 were waited for; matrix products, arithmetic and copies ran while one was open for 4% of the time, Pallas kernels for 0%

commit v1 on v0

v1 whole, which is shorter than its diff:
```python
import math

import jax
import jax.numpy as jnp
from jax import lax
from jax.sharding import PartitionSpec as P

NF = 128
M = 1536
P_SIZE = 32
NB = 32
NSTEPS = 12
PRIME = 65521


def probe_blocks(block_seeds, start_col, number):
    column = (start_col + jnp.arange(number, dtype=jnp.int32))[None, None, :]
    probe_col = jnp.arange(P_SIZE, dtype=jnp.int32)[None, :, None]
    seed = block_seeds[:, None, None]
    inner = seed * (column + 1) % PRIME * (column + 3) % PRIME
    second = seed * (probe_col + 1) % PRIME * (probe_col + 2)
    phase = (inner * (probe_col + 1) + second).astype(jnp.float32)
    phase = phase - jnp.round(phase * (1.0 / PRIME)) * PRIME
    return jnp.cos((2.0 * math.pi / PRIME) * phase).astype(jnp.bfloat16)


def wave(freq, step, sign):
    angle = (math.pi / NF) * (freq[:, None] + 0.5) * step[None, :]
    window = jnp.exp(-math.log(3.0) * step / NB)[None, :]
    both = jnp.stack([jnp.cos(angle) * window, sign * jnp.sin(angle) * window], 1)
    return both.reshape(2 * freq.shape[0], step.shape[0])


def finish(mine, gram):
    highest = lax.Precision.HIGHEST
    scale = jnp.trace(gram) + 1e-06
    current = gram / scale
    eye_mat = jnp.eye(P_SIZE, dtype=jnp.float32)
    inverse = eye_mat
    for repeat in range(NSTEPS):
        weight = 1.5 * eye_mat - 0.5 * jnp.dot(inverse, current, precision=highest)
        current = jnp.dot(current, weight, precision=highest)
        inverse = jnp.dot(weight, inverse, precision=highest)
    factor = math.sqrt(NB * M) / jnp.sqrt(scale)
    return factor * jnp.einsum("pc,pq->cq", mine, inverse, precision=highest)


def shards(damping, block_seeds):
    highest = lax.Precision.HIGHEST
    rows, cols = lax.axis_size("row"), lax.axis_size("col")
    tile, own = damping.shape[0], damping.shape[1]
    strip = M // cols // rows
    steps = jnp.arange(NB, dtype=jnp.float32)
    every = jnp.arange(NF, dtype=jnp.float32)
    mine = (lax.axis_index("row") * own + jnp.arange(own)).astype(jnp.float32)
    amp = math.sqrt(2.0 / NF) / math.sqrt(NB * M)

    probes = probe_blocks(block_seeds, lax.axis_index("col") * tile, tile)
    table = wave(mine, steps, 1.0).astype(jnp.bfloat16)
    mixed = jnp.einsum("kj,jpc->kpc", table, probes, preferred_element_type=jnp.float32)
    mixed = mixed.astype(jnp.bfloat16).reshape(own, 2, P_SIZE, tile)
    part = jnp.einsum("kspc,ckr->rksp", mixed, damping, preferred_element_type=jnp.float32)
    part = part.astype(jnp.bfloat16).reshape(M, 2 * own * P_SIZE)
    part = lax.psum_scatter(part, "col", scatter_dimension=0, tiled=True)
    part = lax.all_to_all(part.reshape(rows, strip, 2 * own, P_SIZE), "row", 0, 0, tiled=True)
    forward = jnp.einsum(
        "aki,ajkp->ijp",
        (amp * wave(every, steps, -1.0)).reshape(rows, 2 * own, NB),
        part.astype(jnp.float32),
        precision=highest,
    )
    forward_b = forward.astype(jnp.bfloat16)
    spread = jnp.einsum(
        "aki,ijp->ajkp",
        (amp * wave(every, steps + 1.0, 1.0)).reshape(rows, 2 * own, NB),
        forward_b.astype(jnp.float32),
        precision=highest,
    ).astype(jnp.bfloat16)
    spread = lax.all_to_all(spread, "row", 0, 0, tiled=True)
    spread = lax.all_gather(spread.reshape(M // cols, 2 * own * P_SIZE), "col", axis=0, tiled=True)
    back = jnp.einsum(
        "ckr,rksp->cksp",
        damping,
        spread.reshape(M, own, 2, P_SIZE),
        preferred_element_type=jnp.float32,
    ).astype(jnp.bfloat16)
    back = lax.all_to_all(back.reshape(rows, strip, 2 * own, P_SIZE), "row", 0, 0, tiled=True)
    backward = jnp.einsum(
        "akj,ackp->jpc",
        wave(every, steps, -1.0).reshape(rows, 2 * own, NB),
        back.astype(jnp.float32),
        precision=highest,
    )
    gram = jnp.einsum("jpc,jqc->pq", backward, backward, precision=highest)
    gram = lax.psum(gram, ("row", "col"))
    block = lax.all_to_all(backward, "row", 0, 2, tiled=True)
    return finish(block[0], gram)[None]


def solution(mesh):
    return jax.shard_map(
        shards,
        mesh=mesh,
        in_specs=(P("col", "row", None), P()),
        out_specs=P("row", "col", None),
        check_vma=False,
    )
```

time: 589 us -> 301 us (0.51); the launches traced: 580 us -> 300 us
  waiting for transfers between devices: 332 us -> 102 us
  local copies, waits for them, and re-layouts: 89.6 us -> 8.49 us
  blocking collectives: 96.7 us -> 143 us
  matrix products: 30.6 us -> 15.2 us
    psum x1 -> x0, waiting for transfers between devices: 283 us -> none  [shards(): full_cols = lax.psum(partial_cols, 'row')]
    reduce_scatter x0 -> x1, waiting for transfers between devices: none -> 87.5 us  [shards(): part = lax.psum_scatter(part, 'col', scatter_dimension=0, tiled=True)]
    all_gather x0 -> x1, blocking collectives: none -> 40.5 us  [shards(): lax.all_gather(spread.reshape(M // cols, 2 * own * P_SIZE), 'col', axis=0...]
    all_to_all x1 -> x2, waiting for transfers between devices: 49.5 us -> 14.8 us  [the longest x1 7.55 us: shards(): lax.all_to_all(part.reshape(rows, strip, 2 * own, P_SIZE), 'row', 0, 0, t...]
    unnamed x35 -> x10, local copies, waits for them, and re-layouts: 34.8 us -> 2.96 us
    all_to_all x0 -> x2, blocking collectives: none -> 28.9 us  [the longest x1 17.3 us: shards(): lax.all_to_all(back.reshape(rows, strip, 2 * own, P_SIZE), 'row', 0, 0, t...]
    dot_general x2 -> x0, local copies, waits for them, and re-layouts: 26.1 us -> none  [hankel_pass(): jnp.einsum(form, window_lags, stack, preferred_element_type=jnp.float32)]
    psum x2 -> x1, blocking collectives: 96.7 us -> 73.9 us  [shards(): gram = lax.psum(gram, ('row', 'col'))]
  transfers between devices with their start and end apart: 2 -> 3, of which waited for: 2 -> 3; matrix products, arithmetic and copies ran while one was open for 4% -> 0% of each run, Pallas kernels for 0% -> 0%
where the time goes in v1:
time: 301 us; the launch traced here: 300 us
  blocking collectives  143 us (48%)
  waiting for transfers between devices  102 us (34%)
  matrix products  15.2 us (5%)
  between operations  14.5 us (5%)
  starting transfers between devices  13.1 us (4%)
  local copies, waits for them, and re-layouts  8.49 us (3%)
  other arithmetic  3.32 us (1%)
    reduce_scatter x1, waiting for transfers between devices, shards(): part = lax.psum_scatter(part, 'col', scatter_dimension=0, tiled=True)  87.5 us
    psum x1, blocking collectives, shards(): gram = lax.psum(gram, ('row', 'col'))  73.9 us
    all_gather x1, blocking collectives, shards(): lax.all_gather(spread.reshape(M // cols, 2 * own * P_SIZE), 'col', axis=0...  40.5 us
    all_to_all x1, blocking collectives, shards(): lax.all_to_all(back.reshape(rows, strip, 2 * own, P_SIZE), 'row', 0, 0, t...  17.3 us
    all_to_all x1, blocking collectives, shards(): spread = lax.all_to_all(spread, 'row', 0, 0, tiled=True)  11.6 us
    all_to_all x1, waiting for transfers between devices, shards(): lax.all_to_all(part.reshape(rows, strip, 2 * own, P_SIZE), 'row', 0, 0, t...  7.55 us
    all_to_all x1, starting transfers between devices, shards(): lax.all_to_all(part.reshape(rows, strip, 2 * own, P_SIZE), 'row', 0, 0, t...  7.48 us
    all_to_all x1, waiting for transfers between devices, shards(): block = lax.all_to_all(backward, 'row', 0, 2, tiled=True)  7.28 us
  transfers between devices with their start and end apart: 3, of which 3 were waited for; matrix products, arithmetic and copies ran while one was open for 0% of the time, Pallas kernels for 0%

profile of v1, /device:TPU:1, one launch (start us, length us, event | category | flops | bytes accessed | tf_op | source)
XLA Modules:
  0.0 300.3 jit_solution(16586436982176172968)
XLA Ops:
  6.7 0.9 fusion.50
  7.6 0.8 add_select_fusion
  8.4 4.6 %convolution_convert_fusion.2 = bf16[8,32,192]{2,0,1:T(8,128)(2,1)S(1)} fusion(bf16[8,32,1]{1,0,2:T(8,128)(2,1)S(1)} %bitcast.141, s32[32,32]{0,1:T(8,128)S(1)} %fusion.50, s32[32]{0:T(128)S(1)} %get-tuple-element.12, s32[32,192]{1,0:T(8,128)S(1)} %add_select_fusion), kind=kOutput, calls=%fused_computation.7 | convolution fusion | flops 4964352 | bytes 127616 | tf_op jit(solution)/shard_map/kj,jpc->kpc/dot_general | solution.py:60
  13.0 0.9 convolution_convert_fusion
  13.9 1.2 copy.76
  15.2 87.5 %reduce-scatter.2.cloned.1.call-done = bf16[192,256]{1,0:T(8,128)(2,1)} async-done(((bf16[1536,256]{1,0:T(8,128)(2,1)}), bf16[192,256]{1,0:T(8,128)(2,1)}) %reduce-scatter.2.cloned.1.call-update) | async-done | bytes 98320 | tf_op jit(solution)/shard_map/reduce_scatter | solution.py:64
  102.7 1.1 reshape.521
  103.9 0.9 reshape.535
  104.8 7.5 %all-to-all-start = ((bf16[32,2,768]{2,1,0:T(2,128)(2,1)}), bf16[32,2,768]{2,1,0:T(2,128)(2,1)S(1)}, u32[]{:S(2)}, u32[]{:S(2)}) async-start(bf16[32,2,768]{2,1,0:T(2,128)(2,1)} %reshape.535), calls=%async_computation.1 | async-start | bytes 196608 | tf_op jit(solution)/shard_map/all_to_all | solution.py:65
  112.3 0.2 fusion.48
  112.8 7.6 %all-to-all-done = bf16[32,2,768]{2,1,0:T(2,128)(2,1)S(1)} async-done(((bf16[32,2,768]{2,1,0:T(2,128)(2,1)}), bf16[32,2,768]{2,1,0:T(2,128)(2,1)S(1)}, u32[]{:S(2)}, u32[]{:S(2)}) %all-to-all-start) | async-done | bytes 98336 | tf_op jit(solution)/shard_map/all_to_all | solution.py:65
  120.4 0.2 reshape.536
  120.6 0.4 fusion.11
  121.0 0.5 fusion.3
  121.5 0.3 copy.81
  121.9 0.3 reshape.537
  122.2 11.6 %all_to_all.30 = bf16[32,2,768]{2,1,0:T(2,128)(2,1)S(1)} all-to-all(bf16[32,2,768]{2,1,0:T(2,128)(2,1)S(1)} %reshape.537), channel_id=1, replica_groups=mesh['row'=32,'col'=8] {'row'}, dimensions={0} | all-to-all | bytes 196608 | tf_op jit(solution)/shard_map/all_to_all | solution.py:79
  133.7 0.2 reshape.538
  133.9 0.3 reshape.522
  134.2 40.5 %all_gather.3 = bf16[1536,256]{1,0:T(8,128)(2,1)S(1)} all-gather(bf16[192,256]{1,0:T(8,128)(2,1)S(1)} %reshape.522), channel_id=1, replica_groups=mesh['row'=32,'col'=8] {'col'}, dimensions={0}, use_global_device_ids=true | all-gather | bytes 884736 | tf_op jit(solution)/shard_map/all_gather | solution.py:80
  174.7 1.2 copy.82
  175.9 2.0 fusion.7
  177.9 0.5 copy.84
  178.3 0.3 reshape.539
  178.7 17.3 %all_to_all.31 = bf16[32,2,768]{2,1,0:T(2,128)(2,1)S(1)} all-to-all(bf16[32,2,768]{2,1,0:T(2,128)(2,1)S(1)} %reshape.539), channel_id=1, replica_groups=mesh['row'=32,'col'=8] {'row'}, dimensions={0} | all-to-all | bytes 196608 | tf_op jit(solution)/shard_map/all_to_all | solution.py:87
  195.9 0.2 reshape.540
  196.2 0.5 convolution_bitcast_fusion
  196.8 0.2 convolution_bitcast_fusion.2
  197.0 73.9 %psum.7 = f32[32,32]{1,0:T(8,128)S(1)} all-reduce(f32[32,32]{1,0:T(8,128)S(1)} %convolution_bitcast_fusion.2), channel_id=1, replica_groups=mesh['row'=32,'col'=8] {'row','col'}, use_global_device_ids=true, to_apply=%region_1.2 | all-reduce | flops 1024 | bytes 8192 | tf_op jit(solution)/shard_map/psum | solution.py:95
  270.9 0.6 select_reduce_fusion
  272.6 0.2 fusion.23
  273.0 0.2 fusion.22
  273.5 0.2 fusion.21
  273.8 0.1 fusion.67
  273.9 0.2 fusion.20
  274.4 0.2 fusion.19
  274.9 0.2 fusion.18
  275.2 0.1 fusion.73
  275.3 0.2 fusion.17
  275.8 0.2 fusion.16
  276.2 0.2 fusion.15
  276.7 0.2 fusion.14
  277.1 0.8 reshape.541
  277.9 5.6 %all-to-all-start.3 = ((f32[32,1,192]{2,1,0:T(1,128)}), f32[32,1,192]{2,1,0:T(1,128)S(1)}, u32[]{:S(2)}, u32[]{:S(2)}) async-start(f32[32,1,192]{2,1,0:T(1,128)} %reshape.541), calls=%async_computation.4 | async-start | bytes 65536 | tf_op jit(solution)/shard_map/all_to_all | solution.py:96
  283.9 7.3 %all-to-all-done.3 = f32[32,1,192]{2,1,0:T(1,128)S(1)} async-done(((f32[32,1,192]{2,1,0:T(1,128)}), f32[32,1,192]{2,1,0:T(1,128)S(1)}, u32[]{:S(2)}, u32[]{:S(2)}) %all-to-all-start.3) | async-done | bytes 24608 | tf_op jit(solution)/shard_map/all_to_all | solution.py:96
  291.2 0.5 broadcast.494
  291.7 0.7 reduce
  292.5 0.9 fusion.12
  (47 shorter events, 4.1 us)
Async XLA Ops:
  6.5 6.5 %copy-start = (bf16[192,4,1536]{2,1,0:T(4,128)(2,1)S(1)}, bf16[192,4,1536]{2,1,0:T(4,128)(2,1)}, u32[]{:S(2)}) copy-start(bf16[192,4,1536]{2,1,0:T(4,128)(2,1)} %param.2) | copy-start | bytes 7077892
  6.5 96.2 %reduce-scatter.2.cloned.1.call-start = ((), (), s32[]{:S(2)}) async-start(), calls=%async_computation.5 | async-start | bytes 884736 | tf_op jit(solution)/shard_map/reduce_scatter | solution.py:64
  104.8 15.6 %all-to-all-start = ((bf16[32,2,768]{2,1,0:T(2,128)(2,1)}), bf16[32,2,768]{2,1,0:T(2,128)(2,1)S(1)}, u32[]{:S(2)}, u32[]{:S(2)}) async-start(bf16[32,2,768]{2,1,0:T(2,128)(2,1)} %reshape.535), calls=%async_computation.1 | async-start | bytes 196608 | tf_op jit(solution)/shard_map/all_to_all | solution.py:65
  277.9 13.3 %all-to-all-start.3 = ((f32[32,1,192]{2,1,0:T(1,128)}), f32[32,1,192]{2,1,0:T(1,128)S(1)}, u32[]{:S(2)}, u32[]{:S(2)}) async-start(f32[32,1,192]{2,1,0:T(1,128)} %reshape.541), calls=%async_computation.4 | async-start | bytes 65536 | tf_op jit(solution)/shard_map/all_to_all | solution.py:96
Sparse Core Ops, SparseCore 0:
  15.2 87.4 reduce-scatter.1

commit v2 on v1

v2 whole, which is shorter than its diff:
```python
import functools
import math

import jax
import jax.numpy as jnp
import numpy as np
from jax import lax
from jax.experimental import pallas as pl
from jax.experimental.pallas import tpu as pltpu
from jax.sharding import PartitionSpec as P

NF = 128
M = 1536
PS = 32
NB = 32
NSTEPS = 12
PRIME = 65521
OWN = 4
KC = 2 * OWN
ROWS = 32
TILE = 192
NX, NY, NZ = 4, 4, 8
CHUNKS = 3
MESH = pl.DeviceIdType.MESH
F32, BF16 = jnp.float32, jnp.bfloat16
HIGHEST = lax.Precision.HIGHEST


def wave(step, sign):
    freq = np.arange(NF)[:, None] + 0.5
    angle = math.pi * freq * step[None, :] / NF
    window = np.exp(-math.log(3.0) * step / NB)[None, :]
    return np.stack([np.cos(angle) * window, sign * np.sin(angle) * window], 1).reshape(2 * NF, len(step))


def halves(table):
    high = table.astype(jnp.bfloat16)
    low = (table - high.astype(np.float64)).astype(jnp.bfloat16)
    return high, low


def tables():
    step = np.arange(NB).astype(np.float64)
    amp = math.sqrt(2.0 / NF) / math.sqrt(NB * M)
    mix = np.repeat(wave(step, 1.0), PS, axis=1).astype(np.float32)
    same = np.eye(2)
    out = (amp * wave(step, -1.0)).reshape(ROWS, KC, NB)
    out = np.einsum("akj,pq->pjaqk", out, same).reshape(2 * NB, ROWS * 2 * KC)
    out = np.concatenate([out, out], axis=1)
    out = np.concatenate(halves(out), axis=0)
    back = (amp * wave(step + 1.0, 1.0)).reshape(ROWS, KC, NB)
    back = np.einsum("akj,pq->apkqj", back, same).reshape(ROWS * 2 * KC, 2 * NB)
    back = np.concatenate(halves(back), axis=1)
    last = wave(step, -1.0).reshape(ROWS // 2, 2, KC, NB // 2, 2)
    last = last.transpose(0, 4, 3, 1, 2)
    last = np.broadcast_to(last[:, :, :, :, None, :], last.shape[:4] + (PS, KC))
    last = last.reshape(ROWS * (NB // 2), 2 * PS * KC).astype(np.float32)
    return mix, out, back, last


def sine_terms():
    t = np.cos(np.pi * (np.arange(400) + 0.5) / 400) * 0.5
    t = t[t > 0]
    u = t * t
    basis = np.stack([u**n for n in range(5)], 1)
    return [float(v) for v in np.linalg.lstsq(basis, np.sin(np.pi * t) / t, rcond=None)[0]]


SINE = sine_terms()


def residue(x):
    q = (x.astype(F32) * (1.0 / PRIME)).astype(jnp.int32)
    r = x - q * PRIME
    r = jnp.where(r < 0, r + PRIME, r)
    return jnp.where(r >= PRIME, r - PRIME, r)


def place():
    r, c = lax.axis_index("row"), lax.axis_index("col")
    return (c // 4) * 4 + r // 8, c % 4, (r // 2) % 4, r % 2


def device(z, x, y, core):
    return ((z % 4) * 8 + y * 2 + core, (z // 4) * 4 + x)


def kernel(seeds, damp_hbm, mix_hbm, out_tab, back_tab, last_hbm, result,
           damp, mix, last, probes, fsend, xrecv, summed, mid, gsend, gbuf,
           hacc, hx, t4h, t4l, bsend, brecv, gz, gyc, gx,
           load_sem, xs_sem, xr_sem, us_sem, ur_sem, gs_sem, gr_sem, as_sem, ar_sem,
           hs_sem, hr_sem, bs_sem, br_sem, qs_sem, qr_sem):
    z, x, y, core = place()
    row, col = lax.axis_index("row"), lax.axis_index("col")
    here = z * 8 + y * 2 + core

    def there(t):
        return device(t // 8, x, (t // 2) % 4, t % 2)

    def beside(d):
        return device(z, (x + d) % NX, y, core)

    loads = [
        pltpu.make_async_copy(mix_hbm.at[pl.ds(pl.multiple_of(row * KC, KC), KC)], mix, load_sem.at[0]),
        pltpu.make_async_copy(damp_hbm, damp, load_sem.at[1]),
        pltpu.make_async_copy(last_hbm.at[pl.ds(pl.multiple_of(row * 16, 16), 16)], last, load_sem.at[2]),
    ]
    for load in loads:
        load.start()
    barrier = pltpu.get_barrier_semaphore()
    for d in range(1, NX):
        pl.semaphore_signal(barrier, inc=1, device_id=beside(d), device_id_type=MESH)

    @pl.loop(1, 64)
    def _(d):
        pl.semaphore_signal(barrier, inc=1, device_id=there((here + d) % 64), device_id_type=MESH)

    column = col * TILE + lax.broadcasted_iota(jnp.int32, (1, TILE), 1)
    pcol = lax.broadcasted_iota(jnp.int32, (PS, 1), 0)
    pone = (pcol + 1).astype(F32)

    @pl.loop(0, NB)
    def _(j):
        s = seeds[j]
        inner = residue(residue(s * (column + 1)) * (column + 3)).astype(F32)
        second = (residue(s * (pcol + 1)) * (pcol + 2)).astype(F32)
        phase = inner * pone + second
        phase = phase - jnp.floor(phase * (1.0 / PRIME) + 0.5) * PRIME
        t = phase * (1.0 / PRIME)
        u = t * t
        poly = SINE[4]
        for n in (3, 2, 1, 0):
            poly = poly * u + SINE[n]
        sine = poly * t
        probes[pl.ds(pl.multiple_of(j * PS, PS), PS), :] = (1.0 - 2.0 * sine * sine).astype(BF16)

    loads[0].wait()
    spread = jnp.broadcast_to(mix[...][None], (PS, KC, NB * PS)).reshape(PS * KC, NB * PS)
    r_idx = lax.broadcasted_iota(jnp.int32, (PS * KC, NB * PS), 0) // KC
    l_idx = lax.broadcasted_iota(jnp.int32, (PS * KC, NB * PS), 1) % PS
    spread = jnp.where(r_idx == l_idx, spread, 0.0).astype(BF16)
    terms = jnp.dot(spread, probes[...], preferred_element_type=F32).astype(BF16)
    wide = lax.broadcasted_iota(jnp.int32, (TILE, TILE * OWN), 1) // OWN
    tall = lax.broadcasted_iota(jnp.int32, (TILE, TILE * OWN), 0)
    expand = jnp.where(wide == tall, 1.0, 0.0).astype(BF16)
    k_row = (lax.broadcasted_iota(jnp.int32, (PS * KC, TILE * OWN), 0) % KC) // 2
    k_lane = lax.broadcasted_iota(jnp.int32, (PS * KC, TILE * OWN), 1) % OWN
    terms = jnp.dot(terms, expand, preferred_element_type=F32)
    terms = jnp.where(k_row == k_lane, terms, 0.0).astype(BF16)

    loads[1].wait()
    pl.semaphore_wait(barrier, 63 + NX - 1)
    sends = []
    for b in range(CHUNKS):
        part = damp[:, :, b * 512 : (b + 1) * 512].reshape(TILE * OWN, 512)
        got = jnp.dot(terms, part, preferred_element_type=F32).astype(BF16)
        for q in range(NX):
            fsend[b, q] = got[:, q * 128 : (q + 1) * 128]
        for d in (2, 1, 3):
            copy = pltpu.make_async_remote_copy(
                src_ref=fsend.at[b, (x + d) % NX], dst_ref=xrecv.at[b, d - 1],
                send_sem=xs_sem.at[b, d - 1], recv_sem=xr_sem.at[b, d - 1],
                device_id=beside(d), device_id_type=MESH)
            copy.start()
            sends.append(copy)

    loads[2].wait()
    same_p = (lax.broadcasted_iota(jnp.int32, (PS, 2 * PS * KC), 0)
              == (lax.broadcasted_iota(jnp.int32, (PS, 2 * PS * KC), 1) // KC) % PS)
    for jj in range(NB // 2):
        line = jnp.where(same_p, last[jj : jj + 1, :], 0.0)
        high = line.astype(BF16)
        t4h[jj * PS : (jj + 1) * PS, :] = high
        t4l[jj * PS : (jj + 1) * PS, :] = (line - high.astype(F32)).astype(BF16)

    for b in range(CHUNKS):
        total = fsend[b, x].astype(F32)
        for d in (1, 3, 2):
            sends[b * 3 + {2: 0, 1: 1, 3: 2}[d]].wait_recv()
            total = total + xrecv[b, d - 1].astype(F32)
        summed[b] = total.astype(BF16)

        @pl.loop(0, 16)
        def _(n):
            unit = (n + z * 2 + core) % 16
            src = summed.at[b, pl.ds(pl.multiple_of(unit * 16, 16), 16), :]
            mine = jnp.logical_and(n == 0, y == b)

            @pl.when(mine)
            def _():
                pltpu.make_async_copy(src, mid.at[here], ur_sem).start()

            @pl.when(jnp.logical_not(mine))
            def _():
                pltpu.make_async_remote_copy(
                    src_ref=src, dst_ref=mid.at[here], send_sem=us_sem, recv_sem=ur_sem,
                    device_id=device(unit // 2, x, b, unit % 2), device_id_type=MESH).start()

    @pl.when(y < CHUNKS)
    def _():
        pltpu.make_async_copy(mid, mid, ur_sem).wait()
        both = jnp.dot(out_tab[...], mid[...].reshape(1024, 128), preferred_element_type=F32)
        forward = (both[: 2 * NB] + both[2 * NB :]).astype(BF16)
        twice = jnp.concatenate([forward, forward], axis=0)
        gsend[...] = jnp.dot(back_tab[...], twice, preferred_element_type=F32).astype(BF16).reshape(ROWS, 16, 128)
        dst = gbuf.at[pl.ds(pl.multiple_of((z * 2 + core) * 16, 16), 16),
                      pl.ds(pl.multiple_of((y * NX + x) * 128, 128), 128)]
        pltpu.make_async_copy(gsend.at[row], dst, gr_sem.at[y]).start()

        @pl.loop(1, 64)
        def _(d):
            t = (here + d) % 64
            pltpu.make_async_remote_copy(
                src_ref=gsend.at[t % 32], dst_ref=dst, send_sem=gs_sem, recv_sem=gr_sem.at[y],
                device_id=there(t), device_id_type=MESH).start()

    gathers = []
    for b in range(CHUNKS):
        block = gbuf.at[:, pl.ds(pl.multiple_of((b * NX + x) * 128, 128), 128)]
        pltpu.make_async_copy(block, block, gr_sem.at[b]).wait()
        for d in (2, 1, 3):
            copy = pltpu.make_async_remote_copy(
                src_ref=block, dst_ref=block, send_sem=as_sem.at[b, d - 1], recv_sem=ar_sem.at[b, d - 1],
                device_id=beside(d), device_id_type=MESH)
            copy.start()
            gathers.append(copy)
    for b in range(CHUNKS):
        for copy in gathers[b * 3 : b * 3 + 3]:
            copy.wait_recv()
        part = damp[:, :, b * 512 : (b + 1) * 512].reshape(TILE * OWN, 512)
        got = lax.dot_general(gbuf[:, b * 512 : (b + 1) * 512], part, (((1,), (1,)), ((), ())),
                              preferred_element_type=F32)
        hacc[...] = got if b == 0 else hacc[...] + got
    back = jnp.where(k_row == k_lane, hacc[...], 0.0).astype(BF16)
    back = lax.dot_general(back, expand, (((1,), (1,)), ((), ())), preferred_element_type=F32).astype(BF16)
    hx[core] = back
    swap = pltpu.make_async_remote_copy(
        src_ref=hx.at[core], dst_ref=hx.at[core], send_sem=hs_sem, recv_sem=hr_sem,
        device_id=device(z, x, y, 1 - core), device_id_type=MESH)
    swap.start()
    swap.wait()

    pair = hx[...].reshape(2 * PS * KC, TILE)
    blocks = jnp.dot(t4h[...], pair, preferred_element_type=F32)
    blocks = blocks + jnp.dot(t4l[...], pair, preferred_element_type=F32)
    bsend[...] = blocks.astype(BF16).reshape(16, PS, TILE)
    chip = (z % 4) * 4 + y
    pltpu.make_async_copy(bsend.at[chip], brecv.at[chip], br_sem).start()

    @pl.loop(1, 16)
    def _(d):
        t = (chip + d) % 16
        pltpu.make_async_remote_copy(
            src_ref=bsend.at[t], dst_ref=brecv.at[chip], send_sem=bs_sem, recv_sem=br_sem,
            device_id=device((z // 4) * 4 + t // 4, x, t % 4, core), device_id_type=MESH).start()

    pltpu.make_async_copy(brecv, brecv, br_sem).wait()
    mine = jnp.sum(brecv[...].astype(F32), axis=0)

    gram = lax.dot_general(mine, mine, (((1,), (1,)), ((), ())), precision=HIGHEST, preferred_element_type=F32)
    gram = jnp.concatenate([gram[n * 8 : n * 8 + 8] for n in range(4)], axis=1)
    for stage, (buf, number, me, who) in enumerate((
        (gz, 8, z, lambda t: device(t, x, y, core)),
        (gyc, 8, y * 2 + core, lambda t: device(z, x, t // 2, t % 2)),
        (gx, 4, x, lambda t: device(z, t, y, core)),
    )):
        buf[me] = gram
        for d in range(1, number):
            pltpu.make_async_remote_copy(
                src_ref=buf.at[me], dst_ref=buf.at[me], send_sem=qs_sem.at[stage], recv_sem=qr_sem.at[stage],
                device_id=who((me + d) % number), device_id_type=MESH).start()
        some = buf.at[pl.ds(0, number - 1)]
        pltpu.make_async_copy(some, some, qr_sem.at[stage]).wait()
        pltpu.make_async_copy(some, some, qs_sem.at[stage]).wait()
        gram = jnp.sum(buf[...], axis=0)
    gram = jnp.concatenate([gram[:, n * 32 : n * 32 + 32] for n in range(4)], axis=0)

    eye = jnp.where(lax.broadcasted_iota(jnp.int32, (PS, PS), 0) == lax.broadcasted_iota(jnp.int32, (PS, PS), 1), 1.0, 0.0)
    scale = jnp.sum(gram * eye, keepdims=True) + 1e-06
    current = gram / scale
    inverse = eye
    for _ in range(NSTEPS):
        weight = 1.5 * eye - 0.5 * jnp.dot(inverse, current, precision=HIGHEST, preferred_element_type=F32)
        current = jnp.dot(current, weight, precision=HIGHEST, preferred_element_type=F32)
        inverse = jnp.dot(weight, inverse, precision=HIGHEST, preferred_element_type=F32)
    answer = lax.dot_general(inverse, mine, (((0,), (0,)), ((), ())), precision=HIGHEST, preferred_element_type=F32)
    result[...] = answer * (math.sqrt(NB * M) / jnp.sqrt(scale))

    for copy in sends + gathers:
        copy.wait_send()
    rest = bsend.at[pl.ds(0, 15)]
    pltpu.make_async_copy(rest, rest, bs_sem).wait()

    @pl.when(y < CHUNKS)
    def _():
        most = mid.at[pl.ds(0, 47)]
        pltpu.make_async_copy(most, most, us_sem).wait()
        most = mid.at[pl.ds(0, 63)]
        pltpu.make_async_copy(most, most, gs_sem).wait()

    @pl.when(y >= CHUNKS)
    def _():
        most = mid.at[pl.ds(0, 48)]
        pltpu.make_async_copy(most, most, us_sem).wait()


def shards(damping, block_seeds):
    mix, out, back, last = tables()
    vmem, anywhere = pl.BlockSpec(memory_space=pltpu.VMEM), pl.BlockSpec(memory_space=pl.ANY)
    dma = pltpu.SemaphoreType.DMA
    turned = pl.pallas_call(
        kernel,
        out_shape=jax.ShapeDtypeStruct((PS, TILE), F32),
        in_specs=[pl.BlockSpec(memory_space=pltpu.SMEM), anywhere, anywhere, vmem, vmem, anywhere],
        out_specs=vmem,
        scratch_shapes=[
            pltpu.VMEM((TILE, OWN, M), BF16),
            pltpu.VMEM((KC, NB * PS), F32),
            pltpu.VMEM((16, 2 * PS * KC), F32),
            pltpu.VMEM((NB * PS, TILE), BF16),
            pltpu.VMEM((CHUNKS, NX, PS * KC, 128), BF16),
            pltpu.VMEM((CHUNKS, NX - 1, PS * KC, 128), BF16),
            pltpu.VMEM((CHUNKS, PS * KC, 128), BF16),
            pltpu.VMEM((64, 16, 128), BF16),
            pltpu.VMEM((ROWS, 16, 128), BF16),
            pltpu.VMEM((PS * KC, M), BF16),
            pltpu.VMEM((PS * KC, TILE * OWN), F32),
            pltpu.VMEM((2, PS * KC, TILE), BF16),
            pltpu.VMEM((512, 512), BF16),
            pltpu.VMEM((512, 512), BF16),
            pltpu.VMEM((16, PS, TILE), BF16),
            pltpu.VMEM((16, PS, TILE), BF16),
            pltpu.VMEM((8, 8, 128), F32),
            pltpu.VMEM((8, 8, 128), F32),
            pltpu.VMEM((4, 8, 128), F32),
            dma((3,)), dma((CHUNKS, 3)), dma((CHUNKS, 3)), dma, dma, dma, dma((CHUNKS,)),
            dma((CHUNKS, 3)), dma((CHUNKS, 3)), dma, dma, dma, dma, dma((3,)), dma((3,)),
        ],
        compiler_params=pltpu.CompilerParams(
            collective_id=0, has_side_effects=True, vmem_limit_bytes=48 << 20),
        name="hankel",
    )(block_seeds, damping, jnp.asarray(mix), jnp.asarray(out), jnp.asarray(back), jnp.asarray(last))
    return turned.T[None]


def solution(mesh):
    return jax.shard_map(
        shards,
        mesh=mesh,
        in_specs=(P("col", "row", None), P()),
        out_specs=P("row", "col", None),
        check_vma=False,
    )
```

time: 301 us -> 82.4 us (0.27)
  blocking collectives: 143 us -> 0 us
  waiting for transfers between devices: 102 us -> 0 us
  Pallas kernels: 0 us -> 74.9 us
  matrix products: 15.2 us -> 0 us
  between operations: 14.5 us -> 0.02 us
  starting transfers between devices: 13.1 us -> 0 us
  other arithmetic: 3.32 us -> 0 us
    reduce_scatter x1 -> x0, waiting for transfers between devices: 87.5 us -> none  [shards(): part = lax.psum_scatter(part, 'col', scatter_dimension=0, tiled=True)]
    pallas_call x0 -> x1, Pallas kernels: none -> 74.9 us  [shards(): pl.pallas_call(kernel, out_shape=jax.ShapeDtypeStruct((PS, TILE), F32), i...]
    psum x1 -> x0, blocking collectives: 73.9 us -> none  [shards(): gram = lax.psum(gram, ('row', 'col'))]
    all_gather x1 -> x0, blocking collectives: 40.5 us -> none  [shards(): lax.all_gather(spread.reshape(M // cols, 2 * own * P_SIZE), 'col', axis=0...]
    all_to_all x2 -> x0, blocking collectives: 28.9 us -> none  [the longest x1 17.3 us: shards(): lax.all_to_all(back.reshape(rows, strip, 2 * own, P_SIZE), 'row', 0, 0, t...]
    dot_general x43 -> x0, matrix products: 15.2 us -> none  [the longest x1 4.6 us: shards(): jnp.einsum('kj,jpc->kpc', table, probes, preferred_element_type=jnp.float32)]
    all_to_all x2 -> x0, waiting for transfers between devices: 14.8 us -> none  [the longest x1 7.55 us: shards(): lax.all_to_all(part.reshape(rows, strip, 2 * own, P_SIZE), 'row', 0, 0, t...]
    all_to_all x2 -> x0, starting transfers between devices: 13.1 us -> none  [the longest x1 7.48 us: shards(): lax.all_to_all(part.reshape(rows, strip, 2 * own, P_SIZE), 'row', 0, 0, t...]
  transfers between devices with their start and end apart: 3 -> 0, of which waited for: 3 -> 0; matrix products, arithmetic and copies ran while one was open for 0% -> 0% of each run, Pallas kernels for 0% -> 0%
where the time goes in v2:
time: 82.4 us; the launch traced here: 82.2 us
  Pallas kernels  74.9 us (91%)
  local copies, waits for them, and re-layouts  7.24 us (9%)
    pallas_call x1, Pallas kernels, shards(): pl.pallas_call(kernel, out_shape=jax.ShapeDtypeStruct((PS, TILE), F32), i...  74.9 us
    unnamed x13, local copies, waits for them, and re-layouts  7.24 us

profile of v2, /device:TPU:1, one launch (start us, length us, event | category | flops | bytes accessed | tf_op | source)
XLA Modules:
  0.0 82.2 jit_solution(13760563881958653778)
XLA Ops:
  0.0 0.0 copy-start
  0.0 1.7 %copy-done = bf16[192,4,1536]{2,1,0:T(4,128)(2,1)S(1)} copy-done((bf16[192,4,1536]{2,1,0:T(4,128)(2,1)S(1)}, bf16[192,4,1536]{2,1,0:T(4,128)(2,1)}, u32[]{:S(2)}) %copy-start) | copy-done | bytes 2359320
  1.7 0.0 copy-start.1
  1.7 1.2 %copy-done.1 = f32[512,512]{1,0:T(8,128)S(1)} copy-done((f32[512,512]{1,0:T(8,128)S(1)}, f32[512,512]{1,0:T(8,128)}, u32[]{:S(2)}) %copy-start.1) | copy-done | bytes 1048600
  2.9 0.0 copy-start.2
  2.9 1.2 %copy-done.2 = f32[256,1024]{1,0:T(8,128)S(1)} copy-done((f32[256,1024]{1,0:T(8,128)S(1)}, f32[256,1024]{1,0:T(8,128)}, u32[]{:S(2)}) %copy-start.2) | copy-done | bytes 1048600
  4.1 0.0 copy-start.3
  4.1 0.9 %copy-done.3 = bf16[128,1024]{1,0:T(8,128)(2,1)S(1)} copy-done((bf16[128,1024]{1,0:T(8,128)(2,1)S(1)}, bf16[128,1024]{1,0:T(8,128)(2,1)}, u32[]{:S(2)}) %copy-start.3) | copy-done | bytes 262168
  5.1 0.0 copy-start.4
  5.1 0.9 %copy-done.4 = bf16[512,128]{1,0:T(8,128)(2,1)S(1)} copy-done((bf16[512,128]{1,0:T(8,128)(2,1)S(1)}, bf16[512,128]{1,0:T(8,128)(2,1)}, u32[]{:S(2)}) %copy-start.4) | copy-done | bytes 131096
  6.0 0.0 copy-start.5
  6.0 0.7 copy-done.5
  6.6 74.9 %hankel.1 = f32[32,192]{1,0:T(8,128)S(1)} custom-call(s32[32]{0:T(128)S(1)} %copy-done.5, bf16[192,4,1536]{2,1,0:T(4,128)(2,1)S(1)} %copy-done, f32[256,1024]{1,0:T(8,128)S(1)} %copy-done.2, bf16[128,1024]{1,0:T(8,128)(2,1)S(1)} %copy-done.3, bf16[512,128]{1,0:T(8,128)(2,1)S(1)} %copy-done.4, f32[512,512]{1,0:T(8,128)S(1)} %copy-done.1), custom_call_target="tpu_custom_call" | custom-call | tf_op jit(solution)/shard_map/hankel/pallas_call | solution.py:311
  81.5 0.6 copy.8
Async XLA Ops:
  0.0 1.7 %copy-start = (bf16[192,4,1536]{2,1,0:T(4,128)(2,1)S(1)}, bf16[192,4,1536]{2,1,0:T(4,128)(2,1)}, u32[]{:S(2)}) copy-start(bf16[192,4,1536]{2,1,0:T(4,128)(2,1)} %damp_hbm.1) | copy-start | bytes 7077892
  1.7 1.2 %copy-start.1 = (f32[512,512]{1,0:T(8,128)S(1)}, f32[512,512]{1,0:T(8,128)}, u32[]{:S(2)}) copy-start(f32[512,512]{1,0:T(8,128)} %constant.11.clone.last_hbm) | copy-start | bytes 3145732
  2.9 1.2 %copy-start.2 = (f32[256,1024]{1,0:T(8,128)S(1)}, f32[256,1024]{1,0:T(8,128)}, u32[]{:S(2)}) copy-start(f32[256,1024]{1,0:T(8,128)} %constant.8.clone.mix_hbm) | copy-start | bytes 3145732
  4.1 0.9 %copy-start.3 = (bf16[128,1024]{1,0:T(8,128)(2,1)S(1)}, bf16[128,1024]{1,0:T(8,128)(2,1)}, u32[]{:S(2)}) copy-start(bf16[128,1024]{1,0:T(8,128)(2,1)} %constant.9.clone.out_tab) | copy-start | bytes 786436
  5.1 0.9 %copy-start.4 = (bf16[512,128]{1,0:T(8,128)(2,1)S(1)}, bf16[512,128]{1,0:T(8,128)(2,1)}, u32[]{:S(2)}) copy-start(bf16[512,128]{1,0:T(8,128)(2,1)} %constant.10.clone.back_tab) | copy-start | bytes 393220
  6.0 0.7 copy-start.5

commit v3 on v2

--- a/solution.py
+++ b/solution.py
@@ -85,14 +85,15 @@
     return ((z % 4) * 8 + y * 2 + core, (z // 4) * 4 + x)
 
 
-def kernel(seeds, damp_hbm, mix_hbm, out_tab, back_tab, last_hbm, result,
-           damp, mix, last, probes, fsend, xrecv, summed, mid, gsend, gbuf,
-           hacc, hx, t4h, t4l, bsend, brecv, gz, gyc, gx,
+def kernel(seeds, damp_hbm, mix_hbm, out_hbm, back_hbm, last_hbm, result,
+           damp, mix, last, out_tab, back_tab, probes, fsend, xrecv, summed, mid, gsend, gbuf,
+           hacc, hx, t4h, t4l, bsend, brecv, gz, gx,
            load_sem, xs_sem, xr_sem, us_sem, ur_sem, gs_sem, gr_sem, as_sem, ar_sem,
            hs_sem, hr_sem, bs_sem, br_sem, qs_sem, qr_sem):
     z, x, y, core = place()
     row, col = lax.axis_index("row"), lax.axis_index("col")
     here = z * 8 + y * 2 + core
+    turn = (y + 8 - z) % NY
 
     def there(t):
         return device(t // 8, x, (t // 2) % 4, t % 2)
@@ -104,12 +105,19 @@
         pltpu.make_async_copy(mix_hbm.at[pl.ds(pl.multiple_of(row * KC, KC), KC)], mix, load_sem.at[0]),
         pltpu.make_async_copy(damp_hbm, damp, load_sem.at[1]),
         pltpu.make_async_copy(last_hbm.at[pl.ds(pl.multiple_of(row * 16, 16), 16)], last, load_sem.at[2]),
+        pltpu.make_async_copy(out_hbm, out_tab, load_sem.at[3]),
+        pltpu.make_async_copy(back_hbm, back_tab, load_sem.at[4]),
     ]
     for load in loads:
         load.start()
     barrier = pltpu.get_barrier_semaphore()
-    for d in range(1, NX):
-        pl.semaphore_signal(barrier, inc=1, device_id=beside(d), device_id_type=MESH)
+
+    @pl.loop(0, 16)
+    def _(d):
+        @pl.when(d % NX > 0)
+        def _():
+            pl.semaphore_signal(barrier, inc=1, device_id=device(z, (x + d) % NX, (y + d // NX) % NY, core),
+                                device_id_type=MESH)
 
     @pl.loop(1, 64)
     def _(d):
@@ -149,7 +157,7 @@
     terms = jnp.where(k_row == k_lane, terms, 0.0).astype(BF16)
 
     loads[1].wait()
-    pl.semaphore_wait(barrier, 63 + NX - 1)
+    pl.semaphore_wait(barrier, 63 + 12)
     sends = []
     for b in range(CHUNKS):
         part = damp[:, :, b * 512 : (b + 1) * 512].reshape(TILE * OWN, 512)
@@ -164,15 +172,17 @@
             copy.start()
             sends.append(copy)
 
-    loads[2].wait()
-    same_p = (lax.broadcasted_iota(jnp.int32, (PS, 2 * PS * KC), 0)
-              == (lax.broadcasted_iota(jnp.int32, (PS, 2 * PS * KC), 1) // KC) % PS)
+    for load in loads[2:]:
+        load.wait()
+    p_lane = (lax.broadcasted_iota(jnp.int32, (PS, 2 * PS * KC), 1) // KC) % PS
+    p_row = lax.broadcasted_iota(jnp.int32, (PS, 2 * PS * KC), 0)
     for jj in range(NB // 2):
-        line = jnp.where(same_p, last[jj : jj + 1, :], 0.0)
-        high = line.astype(BF16)
-        t4h[jj * PS : (jj + 1) * PS, :] = high
-        t4l[jj * PS : (jj + 1) * PS, :] = (line - high.astype(F32)).astype(BF16)
-
+        line = jnp.broadcast_to(last[jj : jj + 1, :], (PS, 2 * PS * KC))
+        high = line.astype(BF16).astype(F32)
+        for keep, rows, at in ((p_row == p_lane, PS, 0), ((p_row == p_lane % 16)[:16], 16, 512)):
+            out = pl.ds(at + jj * rows, rows)
+            t4h[out, :] = jnp.where(keep, high[:rows], 0.0).astype(BF16)
+            t4l[out, :] = jnp.where(keep, (line - high)[:rows], 0.0).astype(BF16)
     for b in range(CHUNKS):
         total = fsend[b, x].astype(F32)
         for d in (1, 3, 2):
@@ -184,7 +194,7 @@
         def _(n):
             unit = (n + z * 2 + core) % 16
             src = summed.at[b, pl.ds(pl.multiple_of(unit * 16, 16), 16), :]
-            mine = jnp.logical_and(n == 0, y == b)
+            mine = jnp.logical_and(n == 0, turn == b)
 
             @pl.when(mine)
             def _():
@@ -194,9 +204,9 @@
             def _():
                 pltpu.make_async_remote_copy(
                     src_ref=src, dst_ref=mid.at[here], send_sem=us_sem, recv_sem=ur_sem,
-                    device_id=device(unit // 2, x, b, unit % 2), device_id_type=MESH).start()
-
-    @pl.when(y < CHUNKS)
+                    device_id=device(unit // 2, x, (b + unit // 2) % NY, unit % 2), device_id_type=MESH).start()
+
+    @pl.when(turn < CHUNKS)
     def _():
         pltpu.make_async_copy(mid, mid, ur_sem).wait()
         both = jnp.dot(out_tab[...], mid[...].reshape(1024, 128), preferred_element_type=F32)
@@ -204,14 +214,14 @@
         twice = jnp.concatenate([forward, forward], axis=0)
         gsend[...] = jnp.dot(back_tab[...], twice, preferred_element_type=F32).astype(BF16).reshape(ROWS, 16, 128)
         dst = gbuf.at[pl.ds(pl.multiple_of((z * 2 + core) * 16, 16), 16),
-                      pl.ds(pl.multiple_of((y * NX + x) * 128, 128), 128)]
-        pltpu.make_async_copy(gsend.at[row], dst, gr_sem.at[y]).start()
+                      pl.ds(pl.multiple_of((turn * NX + x) * 128, 128), 128)]
+        pltpu.make_async_copy(gsend.at[row], dst, gr_sem.at[turn]).start()
 
         @pl.loop(1, 64)
         def _(d):
             t = (here + d) % 64
             pltpu.make_async_remote_copy(
-                src_ref=gsend.at[t % 32], dst_ref=dst, send_sem=gs_sem, recv_sem=gr_sem.at[y],
+                src_ref=gsend.at[t % 32], dst_ref=dst, send_sem=gs_sem, recv_sem=gr_sem.at[turn],
                 device_id=there(t), device_id_type=MESH).start()
 
     gathers = []
@@ -232,7 +242,11 @@
                               preferred_element_type=F32)
         hacc[...] = got if b == 0 else hacc[...] + got
     back = jnp.where(k_row == k_lane, hacc[...], 0.0).astype(BF16)
-    back = lax.dot_general(back, expand, (((1,), (1,)), ((), ())), preferred_element_type=F32).astype(BF16)
+    fold = jnp.concatenate([expand, expand[128:]], axis=0)
+    back = lax.dot_general(back, fold, (((1,), (1,)), ((), ())), preferred_element_type=F32)
+    upper = lax.broadcasted_iota(jnp.int32, (PS * KC, 256), 0) >= PS * KC // 2
+    lane = lax.broadcasted_iota(jnp.int32, (PS * KC, 256), 1)
+    back = jnp.where(jnp.logical_or(lane < 128, upper == (lane >= TILE)), back, 0.0).astype(BF16)
     hx[core] = back
     swap = pltpu.make_async_remote_copy(
         src_ref=hx.at[core], dst_ref=hx.at[core], send_sem=hs_sem, recv_sem=hr_sem,
@@ -240,10 +254,11 @@
     swap.start()
     swap.wait()
 
-    pair = hx[...].reshape(2 * PS * KC, TILE)
-    blocks = jnp.dot(t4h[...], pair, preferred_element_type=F32)
-    blocks = blocks + jnp.dot(t4l[...], pair, preferred_element_type=F32)
-    bsend[...] = blocks.astype(BF16).reshape(16, PS, TILE)
+    for rows, at, to, lanes in ((PS, 0, 0, 0), (16, 512, PS, 128)):
+        pair = hx[:, :, lanes : lanes + 128].reshape(2 * PS * KC, 128)
+        blocks = jnp.dot(t4h[at : at + 16 * rows, :], pair, preferred_element_type=F32)
+        blocks = blocks + jnp.dot(t4l[at : at + 16 * rows, :], pair, preferred_element_type=F32)
+        bsend[:, to : to + rows, :] = blocks.astype(BF16).reshape(16, rows, 128)
     chip = (z % 4) * 4 + y
     pltpu.make_async_copy(bsend.at[chip], brecv.at[chip], br_sem).start()
 
@@ -256,49 +271,81 @@
 
     pltpu.make_async_copy(brecv, brecv, br_sem).wait()
     mine = jnp.sum(brecv[...].astype(F32), axis=0)
-
-    gram = lax.dot_general(mine, mine, (((1,), (1,)), ((), ())), precision=HIGHEST, preferred_element_type=F32)
-    gram = jnp.concatenate([gram[n * 8 : n * 8 + 8] for n in range(4)], axis=1)
-    for stage, (buf, number, me, who) in enumerate((
-        (gz, 8, z, lambda t: device(t, x, y, core)),
-        (gyc, 8, y * 2 + core, lambda t: device(z, x, t // 2, t % 2)),
-        (gx, 4, x, lambda t: device(z, t, y, core)),
+    edge = mine[PS:]
+    low = lax.broadcasted_iota(jnp.int32, (16, 128), 1) < 64
+    edge = jnp.concatenate([jnp.where(low, edge, 0.0), jnp.where(low, pltpu.roll(edge, 64, 1), 0.0)], axis=0)
+    mine = jnp.concatenate([mine[:PS], edge], axis=1)
+
+    group = lax.broadcasted_iota(jnp.int32, (8, 128), 1) // PS
+    gram = lax.dot_general(mine, jnp.concatenate([mine] * 4, axis=0), (((1,), (1,)), ((), ())),
+                           precision=HIGHEST, preferred_element_type=F32)
+    packed = gram[0:8]
+    for n in range(1, 4):
+        packed = jnp.where(group == n, gram[n * 8 : n * 8 + 8], packed)
+    for stage, (buf, me, who) in enumerate((
+        (gz, z * 2 + core, lambda t: device(t // 2, x, y, t % 2)),
+        (gx, x * 4 + y, lambda t: device(z, t // 4, t % 4, core)),
     )):
-        buf[me] = gram
-        for d in range(1, number):
+        buf[me] = packed
+
+        @pl.loop(1, 16)
+        def _(d):
             pltpu.make_async_remote_copy(
                 src_ref=buf.at[me], dst_ref=buf.at[me], send_sem=qs_sem.at[stage], recv_sem=qr_sem.at[stage],
-                device_id=who((me + d) % number), device_id_type=MESH).start()
-        some = buf.at[pl.ds(0, number - 1)]
+                device_id=who((me + d) % 16), device_id_type=MESH).start()
+        some = buf.at[pl.ds(0, 15)]
         pltpu.make_async_copy(some, some, qr_sem.at[stage]).wait()
         pltpu.make_async_copy(some, some, qs_sem.at[stage]).wait()
-        gram = jnp.sum(buf[...], axis=0)
-    gram = jnp.concatenate([gram[:, n * 32 : n * 32 + 32] for n in range(4)], axis=0)
-
-    eye = jnp.where(lax.broadcasted_iota(jnp.int32, (PS, PS), 0) == lax.broadcasted_iota(jnp.int32, (PS, PS), 1), 1.0, 0.0)
-    scale = jnp.sum(gram * eye, keepdims=True) + 1e-06
-    current = gram / scale
+        packed = jnp.sum(buf[...], axis=0)
+
+    turned = [packed] + [pltpu.roll(packed, n * PS, 1) for n in range(1, 4)]
+    strips = []
+    for n in range(4):
+        strip = turned[(4 - n) % 4]
+        for g in range(1, 4):
+            strip = jnp.where(group == g, turned[(g - n) % 4], strip)
+        strips.append(strip)
+    gram = jnp.concatenate(strips, axis=0)
+    s_row = lax.broadcasted_iota(jnp.int32, (PS, 128), 0)
+    s_lane = lax.broadcasted_iota(jnp.int32, (PS, 128), 1)
+    eye = jnp.where(s_row == s_lane % PS, 1.0, 0.0)
+    scale = jnp.sum(jnp.where(s_row == s_lane, gram, 0.0), keepdims=True) + 1e-06
+
+    def left(a):
+        high = a.astype(BF16).astype(F32)
+        lane = lax.broadcasted_iota(jnp.int32, a.shape, 1)
+        return jnp.where(lane < 64, high, a - high).astype(BF16)
+
+    def right(a):
+        high = a.astype(BF16)
+        low = (a - high.astype(F32)).astype(BF16)
+        return jnp.concatenate([high, low, high, low], axis=0)
+
+    square = gram / scale
     inverse = eye
-    for _ in range(NSTEPS):
-        weight = 1.5 * eye - 0.5 * jnp.dot(inverse, current, precision=HIGHEST, preferred_element_type=F32)
-        current = jnp.dot(current, weight, precision=HIGHEST, preferred_element_type=F32)
-        inverse = jnp.dot(weight, inverse, precision=HIGHEST, preferred_element_type=F32)
-    answer = lax.dot_general(inverse, mine, (((0,), (0,)), ((), ())), precision=HIGHEST, preferred_element_type=F32)
-    result[...] = answer * (math.sqrt(NB * M) / jnp.sqrt(scale))
+    for step in range(NSTEPS):
+        weight = 1.5 * eye - 0.5 * square
+        factor = right(weight)
+        both = jnp.dot(left(jnp.concatenate([square, inverse], axis=0)), factor, preferred_element_type=F32)
+        inverse = both[PS:]
+        if step < NSTEPS - 1:
+            square = jnp.dot(left(both[:PS]), factor, preferred_element_type=F32)
+    answer = jnp.dot(left(inverse), right(mine), preferred_element_type=F32)
+    result[...] = answer[:, :TILE] * (math.sqrt(NB * M) / jnp.sqrt(scale))
 
     for copy in sends + gathers:
         copy.wait_send()
     rest = bsend.at[pl.ds(0, 15)]
     pltpu.make_async_copy(rest, rest, bs_sem).wait()
 
-    @pl.when(y < CHUNKS)
+    @pl.when(turn < CHUNKS)
     def _():
         most = mid.at[pl.ds(0, 47)]
         pltpu.make_async_copy(most, most, us_sem).wait()
         most = mid.at[pl.ds(0, 63)]
         pltpu.make_async_copy(most, most, gs_sem).wait()
 
-    @pl.when(y >= CHUNKS)
+    @pl.when(turn >= CHUNKS)
     def _():
         most = mid.at[pl.ds(0, 48)]
         pltpu.make_async_copy(most, most, us_sem).wait()
@@ -311,12 +358,14 @@
     turned = pl.pallas_call(
         kernel,
         out_shape=jax.ShapeDtypeStruct((PS, TILE), F32),
-        in_specs=[pl.BlockSpec(memory_space=pltpu.SMEM), anywhere, anywhere, vmem, vmem, anywhere],
+        in_specs=[pl.BlockSpec(memory_space=pltpu.SMEM), anywhere, anywhere, anywhere, anywhere, anywhere],
         out_specs=vmem,
         scratch_shapes=[
             pltpu.VMEM((TILE, OWN, M), BF16),
             pltpu.VMEM((KC, NB * PS), F32),
             pltpu.VMEM((16, 2 * PS * KC), F32),
+            pltpu.VMEM((4 * NB, 1024), BF16),
+            pltpu.VMEM((512, 4 * NB), BF16),
             pltpu.VMEM((NB * PS, TILE), BF16),
             pltpu.VMEM((CHUNKS, NX, PS * KC, 128), BF16),
             pltpu.VMEM((CHUNKS, NX - 1, PS * KC, 128), BF16),
@@ -325,19 +374,18 @@
             pltpu.VMEM((ROWS, 16, 128), BF16),
             pltpu.VMEM((PS * KC, M), BF16),
             pltpu.VMEM((PS * KC, TILE * OWN), F32),
-            pltpu.VMEM((2, PS * KC, TILE), BF16),
-            pltpu.VMEM((512, 512), BF16),
-            pltpu.VMEM((512, 512), BF16),
-            pltpu.VMEM((16, PS, TILE), BF16),
-            pltpu.VMEM((16, PS, TILE), BF16),
-            pltpu.VMEM((8, 8, 128), F32),
-            pltpu.VMEM((8, 8, 128), F32),
-            pltpu.VMEM((4, 8, 128), F32),
-            dma((3,)), dma((CHUNKS, 3)), dma((CHUNKS, 3)), dma, dma, dma, dma((CHUNKS,)),
-            dma((CHUNKS, 3)), dma((CHUNKS, 3)), dma, dma, dma, dma, dma((3,)), dma((3,)),
+            pltpu.VMEM((2, PS * KC, 256), BF16),
+            pltpu.VMEM((768, 512), BF16),
+            pltpu.VMEM((768, 512), BF16),
+            pltpu.VMEM((16, 48, 128), BF16),
+            pltpu.VMEM((16, 48, 128), BF16),
+            pltpu.VMEM((16, 8, 128), F32),
+            pltpu.VMEM((16, 8, 128), F32),
+            dma((5,)), dma((CHUNKS, 3)), dma((CHUNKS, 3)), dma, dma, dma, dma((CHUNKS,)),
+            dma((CHUNKS, 3)), dma((CHUNKS, 3)), dma, dma, dma, dma, dma((2,)), dma((2,)),
         ],
         compiler_params=pltpu.CompilerParams(
-            collective_id=0, has_side_effects=True, vmem_limit_bytes=48 << 20),
+            collective_id=0, has_side_effects=True, vmem_limit_bytes=62 << 20),
         name="hankel",
     )(block_seeds, damping, jnp.asarray(mix), jnp.asarray(out), jnp.asarray(back), jnp.asarray(last))
     return turned.T[None]

time: 82.4 us -> 69.9 us (0.85)
  Pallas kernels: 74.9 us -> 68.4 us
  local copies, waits for them, and re-layouts: 7.24 us -> 1.38 us
    pallas_call x1, Pallas kernels: 74.9 us -> 68.4 us  [shards(): pl.pallas_call(kernel, out_shape=jax.ShapeDtypeStruct((PS, TILE), F32), i...]
    unnamed x13 -> x1, local copies, waits for them, and re-layouts: 7.24 us -> 1.38 us
where the time goes in v3:
time: 69.9 us; the launch traced here: 69.7 us
  Pallas kernels  68.4 us (98%)
  local copies, waits for them, and re-layouts  1.38 us (2%)
    pallas_call x1, Pallas kernels, shards(): pl.pallas_call(kernel, out_shape=jax.ShapeDtypeStruct((PS, TILE), F32), i...  68.4 us

profile of v3, /device:TPU:1, one launch (start us, length us, event | category | flops | bytes accessed | tf_op | source)
XLA Modules:
  0.0 69.7 jit_solution(198755085916037446)
XLA Ops:
  0.0 68.4 %hankel.1 = f32[32,192]{1,0:T(8,128)} custom-call(s32[32]{0:T(128)} %seeds.1, bf16[192,4,1536]{2,1,0:T(4,128)(2,1)} %damp_hbm.1, f32[256,1024]{1,0:T(8,128)} %constant.8.clone.mix_hbm, bf16[128,1024]{1,0:T(8,128)(2,1)} %constant.9.clone.out_hbm, bf16[512,128]{1,0:T(8,128)(2,1)} %constant.10.clone.back_hbm, f32[512,512]{1,0:T(8,128)} %constant.11.clone.last_hbm), custom_call_target="tpu_custom_call" | custom-call | tf_op jit(solution)/shard_map/hankel/pallas_call | solution.py:358
  68.4 1.4 %copy.8 = f32[1,192,32]{1,2,0:T(8,128)} copy(f32[1,192,32]{1,2,0:T(8,128)} %bitcast.3) | data formatting | bytes 49152

commit v4 on v3

v4 whole, which is shorter than its diff:
```python
import functools
import math

import jax
import jax.numpy as jnp
import numpy as np
from jax import lax
from jax.experimental import pallas as pl
from jax.experimental.pallas import tpu as pltpu
from jax.sharding import PartitionSpec as P

NF = 128
M = 1536
PS = 32
NB = 32
NSTEPS = 12
PRIME = 65521
OWN = 4
KC = 2 * OWN
ROWS = 32
TILE = 192
NX, NY, NZ = 4, 4, 8
CHUNKS = 4
PC = PS // CHUNKS
CR = PC * KC
BLOCKS = 3
STRIP = BLOCKS * 128
MESH = pl.DeviceIdType.MESH
F32, BF16 = jnp.float32, jnp.bfloat16
HIGHEST = lax.Precision.HIGHEST


def wave(step, sign):
    freq = np.arange(NF)[:, None] + 0.5
    angle = math.pi * freq * step[None, :] / NF
    window = np.exp(-math.log(3.0) * step / NB)[None, :]
    return np.stack([np.cos(angle) * window, sign * np.sin(angle) * window], 1).reshape(2 * NF, len(step))


def halves(table):
    high = table.astype(jnp.bfloat16)
    low = (table - high.astype(np.float64)).astype(jnp.bfloat16)
    return high, low


def tables():
    step = np.arange(NB).astype(np.float64)
    amp = math.sqrt(2.0 / NF) / math.sqrt(NB * M)
    mix = np.repeat(wave(step, 1.0), PS, axis=1).astype(np.float32)
    same = np.eye(2)
    out = (amp * wave(step, -1.0)).reshape(ROWS, KC, NB)
    out = np.einsum("akj,pq->pjaqk", out, same).reshape(2 * NB, ROWS * 2 * KC)
    out = np.concatenate([out, out], axis=1)
    out = np.concatenate(halves(out), axis=0)
    back = (amp * wave(step + 1.0, 1.0)).reshape(ROWS, KC, NB)
    back = np.einsum("akj,pq->apkqj", back, same).reshape(ROWS * 2 * KC, 2 * NB)
    back = np.concatenate(halves(back), axis=1)
    last = wave(step, -1.0).reshape(ROWS // 2, 2, KC, NB // 2, 2)
    last = last.transpose(0, 4, 3, 1, 2)
    last = np.broadcast_to(last[:, :, :, :, None, :], last.shape[:4] + (PC, KC))
    last = last.reshape(ROWS * (NB // 2), 2 * CR).astype(np.float32)
    return mix, out, back, last


def sine_terms():
    t = np.cos(np.pi * (np.arange(400) + 0.5) / 400) * 0.5
    t = t[t > 0]
    u = t * t
    basis = np.stack([u**n for n in range(5)], 1)
    return [float(v) for v in np.linalg.lstsq(basis, np.sin(np.pi * t) / t, rcond=None)[0]]


SINE = sine_terms()


def residue(x):
    q = (x.astype(F32) * (1.0 / PRIME)).astype(jnp.int32)
    r = x - q * PRIME
    r = jnp.where(r < 0, r + PRIME, r)
    return jnp.where(r >= PRIME, r - PRIME, r)


FAR4 = (2, 1, 3, 0)
FAR8 = (4, 3, 5, 2, 6, 1, 7, 0)


def rem(a, n):
    return lax.rem(a, jnp.int32(n))


def div(a, n):
    return lax.div(a, jnp.int32(n))


def far8(k):
    half = div(k + 1, 2)
    return 4 + half - 2 * half * rem(k, 2)


def place():
    r, c = lax.axis_index("row"), lax.axis_index("col")
    return div(c, 4) * 4 + div(r, 8), rem(c, 4), rem(div(r, 2), 4), rem(r, 2)


def device(z, x, y, core):
    return (rem(z, 4) * 8 + y * 2 + core, div(z, 4) * 4 + x)


def kernel(seeds, damp_hbm, mix_hbm, out_hbm, back_hbm, last_hbm, result,
           damp, flat, mix, last, out_tab, back_tab, probes, fsend, xrecv, summed, mid, gsend, gbuf,
           hx, bsend, brecv, gz, gx,
           ready, load_sem, xs_sem, xr_sem, us_sem, ur_sem, gs_sem, gr_sem, as_sem, ar_sem,
           hs_sem, hr_sem, bs_sem, br_sem, qs_sem, qr_sem):
    z, x, y, core = place()
    row, col = lax.axis_index("row"), lax.axis_index("col")
    here = z * 8 + y * 2 + core
    my_chunk, my_pair, my_block = core * 2 + rem(z, 2), div(z, 2), rem(y + 4 - div(z, 2), NY)

    def beside(d):
        return device(z, rem(x + d, NX), y, core)

    def plane(dy, dc):
        return device(z, x, rem(y + dy, NY), core if dc == 0 else 1 - core)

    around = [(dy, dc) for dy in FAR4 for dc in (1, 0) if dy or dc]

    loads = [
        pltpu.make_async_copy(damp_hbm, damp, load_sem.at[1]),
        pltpu.make_async_copy(mix_hbm.at[pl.ds(pl.multiple_of(row * KC, KC), KC)], mix, load_sem.at[0]),
        pltpu.make_async_copy(last_hbm.at[pl.ds(pl.multiple_of(row * 16, 16), 16)], last, load_sem.at[2]),
        pltpu.make_async_copy(out_hbm, out_tab, load_sem.at[3]),
        pltpu.make_async_copy(back_hbm, back_tab, load_sem.at[4]),
    ]
    barrier = pltpu.get_barrier_semaphore()
    for d in FAR8[:-1]:
        pl.semaphore_signal(barrier, inc=1, device_id=device(rem(z + d, NZ), x, y, core), device_id_type=MESH)
    for dy, dc in around:
        pl.semaphore_signal(barrier, inc=1, device_id=plane(dy, dc), device_id_type=MESH)
    for d in FAR4[:-1]:
        pl.semaphore_signal(barrier, inc=1, device_id=beside(d), device_id_type=MESH)
    for load in loads:
        load.start()

    column = col * TILE + lax.broadcasted_iota(jnp.int32, (1, TILE), 1)
    pcol = lax.broadcasted_iota(jnp.int32, (PS, 1), 0)
    pone = (pcol + 1).astype(F32)

    @pl.loop(0, NB)
    def _(j):
        s = seeds[j]
        inner = residue(residue(s * (column + 1)) * (column + 3)).astype(F32)
        second = (residue(s * (pcol + 1)) * (pcol + 2)).astype(F32)
        phase = inner * pone + second
        phase = phase - jnp.floor(phase * (1.0 / PRIME) + 0.5) * PRIME
        t = phase * (1.0 / PRIME)
        u = t * t
        poly = SINE[4]
        for n in (3, 2, 1, 0):
            poly = poly * u + SINE[n]
        sine = poly * t
        probes[pl.ds(pl.multiple_of(j * PS, PS), PS), :] = (1.0 - 2.0 * sine * sine).astype(BF16)

    loads[1].wait()
    spread = jnp.broadcast_to(mix[...][None], (PS, KC, NB * PS)).reshape(PS * KC, NB * PS)
    r_idx = lax.broadcasted_iota(jnp.int32, (PS * KC, NB * PS), 0) // KC
    l_idx = lax.broadcasted_iota(jnp.int32, (PS * KC, NB * PS), 1) % PS
    spread = jnp.where(r_idx == l_idx, spread, 0.0).astype(BF16)
    terms = jnp.dot(spread, probes[...], preferred_element_type=F32).astype(BF16)
    wide = lax.broadcasted_iota(jnp.int32, (TILE, TILE * OWN), 1) // OWN
    tall = lax.broadcasted_iota(jnp.int32, (TILE, TILE * OWN), 0)
    expand = jnp.where(wide == tall, 1.0, 0.0).astype(BF16)
    k_row = (lax.broadcasted_iota(jnp.int32, (PS * KC, TILE * OWN), 0) % KC) // 2
    k_lane = lax.broadcasted_iota(jnp.int32, (PS * KC, TILE * OWN), 1) % OWN
    terms = jnp.dot(terms, expand, preferred_element_type=F32)
    terms = jnp.where(k_row == k_lane, terms, 0.0).astype(BF16)

    loads[0].wait()
    for n in range(3):
        flat[:, n * 512 : (n + 1) * 512] = damp[:, :, n * 512 : (n + 1) * 512].reshape(TILE * OWN, 512)
    for load in loads[2:]:
        load.wait()
    sends = []
    for b in range(CHUNKS):
        got = jnp.dot(terms[b * CR : (b + 1) * CR], flat[...], preferred_element_type=F32).astype(BF16)
        for q in range(NX):
            fsend[b, q] = got[:, q * STRIP : (q + 1) * STRIP]
        if b == 0:
            pl.semaphore_wait(barrier, 7 + 7 + NX - 1)
        for d in (2, 1, 3):
            copy = pltpu.make_async_remote_copy(
                src_ref=fsend.at[b, rem(x + d, NX)], dst_ref=xrecv.at[b, d - 1],
                send_sem=xs_sem.at[b, d - 1], recv_sem=xr_sem.at[b, d - 1],
                device_id=beside(d), device_id_type=MESH)
            copy.start()
            sends.append(copy)
        if b == 0:
            for dy, dc in around:
                pl.semaphore_signal(ready, inc=1, device_id=plane(dy, dc), device_id_type=MESH)

    pl.semaphore_wait(ready, 7)
    for b in range(CHUNKS):
        total = fsend[b, x].astype(F32)
        for d, at in ((1, 1), (3, 2), (2, 0)):
            sends[b * 3 + at].wait_recv()
            total = total + xrecv[b, d - 1].astype(F32)
        summed[b] = total.astype(BF16)

        @pl.loop(0, 4)
        def _(k):
            pair = rem(div(z, 2) + 2 + k, 4)
            to_z, to_core = pair * 2 + b % 2, b // 2
            for block in range(BLOCKS):
                src = summed.at[b, pl.ds(pl.multiple_of(pair * 16, 16), 16), pl.ds(block * 128, 128)]
                to_y = rem(pair + block, NY)
                mine = jnp.logical_and(jnp.logical_and(to_z == z, to_y == y), to_core == core)

                @pl.when(mine)
                def _():
                    pltpu.make_async_copy(src, mid.at[here], ur_sem).start()

                @pl.when(jnp.logical_not(mine))
                def _():
                    pltpu.make_async_remote_copy(
                        src_ref=src, dst_ref=mid.at[here], send_sem=us_sem, recv_sem=ur_sem,
                        device_id=device(to_z, x, to_y, to_core), device_id_type=MESH).start()

    @pl.when(my_block < BLOCKS)
    def _():
        pltpu.make_async_copy(mid, mid, ur_sem).wait()
        both = jnp.dot(out_tab[...], mid[...].reshape(1024, 128), preferred_element_type=F32)
        forward = (both[: 2 * NB] + both[2 * NB :]).astype(BF16)
        twice = jnp.concatenate([forward, forward], axis=0)
        gsend[...] = jnp.dot(back_tab[...], twice, preferred_element_type=F32).astype(BF16).reshape(ROWS, 16, 128)
        dst = gbuf.at[pl.ds(pl.multiple_of(my_chunk * CR + my_pair * 16, 16), 16),
                      pl.ds(pl.multiple_of(x * STRIP + my_block * 128, 128), 128)]
        pltpu.make_async_copy(gsend.at[row], dst, gr_sem.at[my_chunk]).start()

        @pl.loop(0, NZ)
        def _(k):
            to_z = rem(z + far8(k), NZ)

            def send(dy, dc):
                to_y, to_core = rem(y + dy, NY), core if dc == 0 else 1 - core
                to = device(to_z, x, to_y, to_core)
                pltpu.make_async_remote_copy(
                    src_ref=gsend.at[to[0]], dst_ref=dst, send_sem=gs_sem, recv_sem=gr_sem.at[my_chunk],
                    device_id=to, device_id_type=MESH).start()

            for dy, dc in around:
                send(dy, dc)

            @pl.when(k < NZ - 1)
            def _():
                send(0, 0)

    gathers, swaps = [], []
    for b in range(CHUNKS):
        block = gbuf.at[pl.ds(b * CR, CR), pl.ds(pl.multiple_of(x * STRIP, 128), STRIP)]
        pltpu.make_async_copy(block, block, gr_sem.at[b]).wait()
        for d in (2, 1, 3):
            copy = pltpu.make_async_remote_copy(
                src_ref=block, dst_ref=block, send_sem=as_sem.at[b, d - 1], recv_sem=ar_sem.at[b, d - 1],
                device_id=beside(d), device_id_type=MESH)
            copy.start()
            gathers.append(copy)
    fold = jnp.concatenate([expand, jnp.zeros((256 - TILE, TILE * OWN), BF16)], axis=0)
    own_k = (k_row == k_lane)[:CR]
    lines = jnp.broadcast_to(last[...][:, None, :], (NB // 2, PC, 2 * CR)).reshape(NB // 2 * PC, 2 * CR)
    p_row = lax.broadcasted_iota(jnp.int32, lines.shape, 0) % PC
    p_lane = (lax.broadcasted_iota(jnp.int32, lines.shape, 1) // KC) % PC
    lines = jnp.where(p_row == p_lane, lines, 0.0)
    high = lines.astype(BF16)
    lines = jnp.concatenate([high, (lines - high.astype(F32)).astype(BF16)], axis=1)
    chip = rem(z, 4) * 4 + y

    def swap_of(b):
        for copy in gathers[b * 3 : b * 3 + 3]:
            copy.wait_recv()
        got = lax.dot_general(gbuf[b * CR : (b + 1) * CR, :], flat[...], (((1,), (1,)), ((), ())),
                              preferred_element_type=F32)
        got = jnp.where(own_k, got, 0.0).astype(BF16)
        hx[b, core] = lax.dot_general(got, fold, (((1,), (1,)), ((), ())), preferred_element_type=F32).astype(BF16)
        swap = pltpu.make_async_remote_copy(
            src_ref=hx.at[b, core], dst_ref=hx.at[b, core], send_sem=hs_sem.at[b], recv_sem=hr_sem.at[b],
            device_id=device(z, x, y, 1 - core), device_id_type=MESH)
        swap.start()
        swaps.append(swap)

    def blocks_of(b):
        swaps[b].wait_recv()
        pair = hx[b].reshape(2 * CR, 256)
        got = jnp.dot(lines, jnp.concatenate([pair, pair], axis=0), preferred_element_type=F32)
        got = jnp.concatenate([got[:, :128].reshape(16, PC, 128), got[:, 128:].reshape(16, PC, 128)], axis=1)
        bsend[b] = got.astype(BF16)
        pltpu.make_async_copy(bsend.at[b, chip], brecv.at[b, chip], br_sem.at[b]).start()

        @pl.loop(0, 4)
        def _(k):
            low = rem(rem(z, 4) + 2 + k, 4)
            for dy in FAR4:
                to_y = rem(y + dy, NY)

                def send():
                    pltpu.make_async_remote_copy(
                        src_ref=bsend.at[b, low * 4 + to_y], dst_ref=brecv.at[b, chip],
                        send_sem=bs_sem.at[b], recv_sem=br_sem.at[b],
                        device_id=device(div(z, 4) * 4 + low, x, to_y, core), device_id_type=MESH).start()

                if dy:
                    send()
                else:
                    pl.when(k != 2)(send)

    for b in range(CHUNKS):
        swap_of(b)
        if b:
            blocks_of(b - 1)
    blocks_of(CHUNKS - 1)
    mine = []
    for b in range(CHUNKS):
        pltpu.make_async_copy(brecv.at[b], brecv.at[b], br_sem.at[b]).wait()
        got = jnp.sum(brecv[b].astype(F32), axis=0)
        mine.append(jnp.concatenate([got[:PC], got[PC:]], axis=1))
    mine = jnp.concatenate(mine, axis=0)

    group = lax.broadcasted_iota(jnp.int32, (8, 128), 1) // PS
    gram = lax.dot_general(mine, jnp.concatenate([mine] * 4, axis=0), (((1,), (1,)), ((), ())),
                           precision=HIGHEST, preferred_element_type=F32)
    packed = gram[0:8]
    for n in range(1, 4):
        packed = jnp.where(group == n, gram[n * 8 : n * 8 + 8], packed)

    def add_up(buf, stage):
        some = buf.at[pl.ds(0, 15)]
        pltpu.make_async_copy(some, some, qr_sem.at[stage]).wait()
        return jnp.sum(buf[...], axis=0)

    def share(buf, me, stage, to):
        pltpu.make_async_remote_copy(
            src_ref=buf.at[me], dst_ref=buf.at[me], send_sem=qs_sem.at[stage], recv_sem=qr_sem.at[stage],
            device_id=to, device_id_type=MESH).start()

    gz[z * 2 + core] = packed
    for d in FAR8:
        for dc in (1, 0):
            if d or dc:
                share(gz, z * 2 + core, 0, device(rem(z + d, NZ), x, y, core if dc == 0 else 1 - core))
    packed = add_up(gz, 0)
    gx[x * 4 + y] = packed
    for dx in FAR4:
        for dy in FAR4:
            if dx or dy:
                share(gx, x * 4 + y, 1, device(z, rem(x + dx, NX), rem(y + dy, NY), core))
    packed = add_up(gx, 1)

    turned = [packed] + [pltpu.roll(packed, n * PS, 1) for n in range(1, 4)]
    strips = []
    for n in range(4):
        strip = turned[(4 - n) % 4]
        for g in range(1, 4):
            strip = jnp.where(group == g, turned[(g - n) % 4], strip)
        strips.append(strip)
    gram = jnp.concatenate(strips, axis=0)
    s_row = lax.broadcasted_iota(jnp.int32, (PS, 128), 0)
    s_lane = lax.broadcasted_iota(jnp.int32, (PS, 128), 1)
    eye = jnp.where(s_row == s_lane % PS, 1.0, 0.0)
    scale = jnp.sum(jnp.where(s_row == s_lane, gram, 0.0), keepdims=True) + 1e-06

    def left(a):
        high = a.astype(BF16).astype(F32)
        lane = lax.broadcasted_iota(jnp.int32, a.shape, 1)
        return jnp.where(lane < 64, high, a - high).astype(BF16)

    def right(a):
        high = a.astype(BF16)
        low = (a - high.astype(F32)).astype(BF16)
        return jnp.concatenate([high, low, high, low], axis=0)

    square = gram / scale
    inverse = eye
    for step in range(NSTEPS):
        weight = 1.5 * eye - 0.5 * square
        factor = right(weight)
        both = jnp.dot(left(jnp.concatenate([square, inverse], axis=0)), factor, preferred_element_type=F32)
        inverse = both[PS:]
        if step < NSTEPS - 1:
            square = jnp.dot(left(both[:PS]), factor, preferred_element_type=F32)
    answer = jnp.dot(left(inverse), right(mine), preferred_element_type=F32)
    result[...] = answer[:, :TILE] * (math.sqrt(NB * M) / jnp.sqrt(scale))

    for copy in sends + gathers + swaps:
        copy.wait_send()
    for stage, buf in enumerate((gz, gx)):
        some = buf.at[pl.ds(0, 15)]
        pltpu.make_async_copy(some, some, qs_sem.at[stage]).wait()
    for b in range(CHUNKS):
        rest = bsend.at[b, pl.ds(0, 15)]
        pltpu.make_async_copy(rest, rest, bs_sem.at[b]).wait()

    @pl.when(my_block < BLOCKS)
    def _():
        most = mid.at[pl.ds(0, 47)]
        pltpu.make_async_copy(most, most, us_sem).wait()
        most = mid.at[pl.ds(0, 63)]
        pltpu.make_async_copy(most, most, gs_sem).wait()

    @pl.when(my_block >= BLOCKS)
    def _():
        most = mid.at[pl.ds(0, 48)]
        pltpu.make_async_copy(most, most, us_sem).wait()


def shards(damping, block_seeds):
    mix, out, back, last = tables()
    vmem, anywhere = pl.BlockSpec(memory_space=pltpu.VMEM), pl.BlockSpec(memory_space=pl.ANY)
    dma = pltpu.SemaphoreType.DMA
    turned = pl.pallas_call(
        kernel,
        out_shape=jax.ShapeDtypeStruct((PS, TILE), F32),
        in_specs=[pl.BlockSpec(memory_space=pltpu.SMEM)] + [anywhere] * 5,
        out_specs=vmem,
        scratch_shapes=[
            pltpu.VMEM((TILE, OWN, M), BF16),
            pltpu.VMEM((TILE * OWN, M), BF16),
            pltpu.VMEM((KC, NB * PS), F32),
            pltpu.VMEM((16, 2 * CR), F32),
            pltpu.VMEM((4 * NB, 1024), BF16),
            pltpu.VMEM((512, 4 * NB), BF16),
            pltpu.VMEM((NB * PS, TILE), BF16),
            pltpu.VMEM((CHUNKS, NX, CR, STRIP), BF16),
            pltpu.VMEM((CHUNKS, NX - 1, CR, STRIP), BF16),
            pltpu.VMEM((CHUNKS, CR, STRIP), BF16),
            pltpu.VMEM((64, 16, 128), BF16),
            pltpu.VMEM((ROWS, 16, 128), BF16),
            pltpu.VMEM((PS * KC, M), BF16),
            pltpu.VMEM((CHUNKS, 2, CR, 256), BF16),
            pltpu.VMEM((CHUNKS, 16, 16, 128), BF16),
            pltpu.VMEM((CHUNKS, 16, 16, 128), BF16),
            pltpu.VMEM((16, 8, 128), F32),
            pltpu.VMEM((16, 8, 128), F32),
            pltpu.SemaphoreType.REGULAR, dma((5,)), dma((CHUNKS, 3)), dma((CHUNKS, 3)), dma, dma, dma,
            dma((CHUNKS,)), dma((CHUNKS, 3)), dma((CHUNKS, 3)), dma((CHUNKS,)), dma((CHUNKS,)),
            dma((CHUNKS,)), dma((CHUNKS,)), dma((2,)), dma((2,)),
        ],
        compiler_params=pltpu.CompilerParams(
            collective_id=0, has_side_effects=True, vmem_limit_bytes=62 << 20),
        name="hankel",
    )(block_seeds, damping, jnp.asarray(mix), jnp.asarray(out), jnp.asarray(back), jnp.asarray(last))
    return turned.T[None]


def solution(mesh):
    return jax.shard_map(
        shards,
        mesh=mesh,
        in_specs=(P("col", "row", None), P()),
        out_specs=P("row", "col", None),
        check_vma=False,
    )
```

time: 69.9 us -> 62.5 us (0.89)
  Pallas kernels: 68.4 us -> 61 us
    pallas_call x1, Pallas kernels: 68.4 us -> 61 us  [shards(): pl.pallas_call(kernel, out_shape=jax.ShapeDtypeStruct((PS, TILE), F32), i...]
where the time goes in v4:
time: 62.5 us; the launch traced here: 62.4 us
  Pallas kernels  61 us (98%)
  local copies, waits for them, and re-layouts  1.38 us (2%)
    pallas_call x1, Pallas kernels, shards(): pl.pallas_call(kernel, out_shape=jax.ShapeDtypeStruct((PS, TILE), F32), i...  61 us
    unnamed x1, local copies, waits for them, and re-layouts  1.38 us

profile of v4, /device:TPU:1, one launch (start us, length us, event | category | flops | bytes accessed | tf_op | source)
XLA Modules:
  0.0 62.4 jit_solution(10101601376109260291)
XLA Ops:
  0.0 61.0 %hankel.1 = f32[32,192]{1,0:T(8,128)} custom-call(s32[32]{0:T(128)} %seeds.1, bf16[192,4,1536]{2,1,0:T(4,128)(2,1)} %damp_hbm.1, f32[256,1024]{1,0:T(8,128)} %constant.8.clone.mix_hbm, bf16[128,1024]{1,0:T(8,128)(2,1)} %constant.9.clone.out_hbm, bf16[512,128]{1,0:T(8,128)(2,1)} %constant.10.clone.back_hbm, f32[512,128]{1,0:T(8,128)} %constant.11.clone.last_hbm), custom_call_target="tpu_custom_call" | custom-call | tf_op jit(solution)/shard_map/hankel/pallas_call | solution.py:417
  61.0 1.4 %copy.8 = f32[1,192,32]{1,2,0:T(8,128)} copy(f32[1,192,32]{1,2,0:T(8,128)} %bitcast.3) | data formatting | bytes 49152

commit v5 on v4

--- a/solution.py
+++ b/solution.py
@@ -106,8 +106,8 @@
     return (rem(z, 4) * 8 + y * 2 + core, div(z, 4) * 4 + x)
 
 
-def kernel(seeds, damp_hbm, mix_hbm, out_hbm, back_hbm, last_hbm, result,
-           damp, flat, mix, last, out_tab, back_tab, probes, fsend, xrecv, summed, mid, gsend, gbuf,
+def kernel(seeds_hbm, damp_hbm, mix_hbm, out_hbm, back_hbm, last_hbm, result,
+           seeds, damp, flat, mix, last, out_tab, back_tab, probes, fsend, xrecv, summed, mid, gsend, gbuf,
            hx, bsend, brecv, gz, gx,
            ready, load_sem, xs_sem, xr_sem, us_sem, ur_sem, gs_sem, gr_sem, as_sem, ar_sem,
            hs_sem, hr_sem, bs_sem, br_sem, qs_sem, qr_sem):
@@ -131,6 +131,9 @@
         pltpu.make_async_copy(out_hbm, out_tab, load_sem.at[3]),
         pltpu.make_async_copy(back_hbm, back_tab, load_sem.at[4]),
     ]
+    seeding = pltpu.make_async_copy(seeds_hbm, seeds, load_sem.at[5])
+    seeding.start()
+    loads[0].start()
     barrier = pltpu.get_barrier_semaphore()
     for d in FAR8[:-1]:
         pl.semaphore_signal(barrier, inc=1, device_id=device(rem(z + d, NZ), x, y, core), device_id_type=MESH)
@@ -138,8 +141,9 @@
         pl.semaphore_signal(barrier, inc=1, device_id=plane(dy, dc), device_id_type=MESH)
     for d in FAR4[:-1]:
         pl.semaphore_signal(barrier, inc=1, device_id=beside(d), device_id_type=MESH)
-    for load in loads:
+    for load in loads[1:]:
         load.start()
+    seeding.wait()
 
     column = col * TILE + lax.broadcasted_iota(jnp.int32, (1, TILE), 1)
     pcol = lax.broadcasted_iota(jnp.int32, (PS, 1), 0)
@@ -181,14 +185,17 @@
         load.wait()
     sends = []
     for b in range(CHUNKS):
-        got = jnp.dot(terms[b * CR : (b + 1) * CR], flat[...], preferred_element_type=F32).astype(BF16)
-        for q in range(NX):
-            fsend[b, q] = got[:, q * STRIP : (q + 1) * STRIP]
-        if b == 0:
-            pl.semaphore_wait(barrier, 7 + 7 + NX - 1)
-        for d in (2, 1, 3):
+        for d in FAR4:
+            q = rem(x + d, NX)
+            part = flat[:, pl.ds(pl.multiple_of(q * STRIP, 128), STRIP)]
+            got = jnp.dot(terms[b * CR : (b + 1) * CR], part, preferred_element_type=F32)
+            fsend[b, q] = got.astype(BF16)
+            if d == 0:
+                continue
+            if b == 0 and d == FAR4[0]:
+                pl.semaphore_wait(barrier, 7 + 7 + NX - 1)
             copy = pltpu.make_async_remote_copy(
-                src_ref=fsend.at[b, rem(x + d, NX)], dst_ref=xrecv.at[b, d - 1],
+                src_ref=fsend.at[b, q], dst_ref=xrecv.at[b, d - 1],
                 send_sem=xs_sem.at[b, d - 1], recv_sem=xr_sem.at[b, d - 1],
                 device_id=beside(d), device_id_type=MESH)
             copy.start()
@@ -274,10 +281,13 @@
     chip = rem(z, 4) * 4 + y
 
     def swap_of(b):
-        for copy in gathers[b * 3 : b * 3 + 3]:
-            copy.wait_recv()
-        got = lax.dot_general(gbuf[b * CR : (b + 1) * CR, :], flat[...], (((1,), (1,)), ((), ())),
-                              preferred_element_type=F32)
+        got = jnp.zeros((CR, TILE * OWN), F32)
+        for d, at in ((0, None), (1, 1), (3, 2), (2, 0)):
+            if d:
+                gathers[b * 3 + at].wait_recv()
+            strip = pl.ds(pl.multiple_of(rem(x + NX - d, NX) * STRIP, 128), STRIP)
+            got = got + lax.dot_general(gbuf[b * CR : (b + 1) * CR, strip], flat[:, strip],
+                                        (((1,), (1,)), ((), ())), preferred_element_type=F32)
         got = jnp.where(own_k, got, 0.0).astype(BF16)
         hx[b, core] = lax.dot_general(got, fold, (((1,), (1,)), ((), ())), preferred_element_type=F32).astype(BF16)
         swap = pltpu.make_async_remote_copy(
@@ -345,13 +355,34 @@
         for dc in (1, 0):
             if d or dc:
                 share(gz, z * 2 + core, 0, device(rem(z + d, NZ), x, y, core if dc == 0 else 1 - core))
+    for copy in sends + gathers + swaps:
+        copy.wait_send()
+
+    @pl.when(my_block < BLOCKS)
+    def _():
+        most = mid.at[pl.ds(0, 47)]
+        pltpu.make_async_copy(most, most, us_sem).wait()
+        most = mid.at[pl.ds(0, 63)]
+        pltpu.make_async_copy(most, most, gs_sem).wait()
+
+    @pl.when(my_block >= BLOCKS)
+    def _():
+        most = mid.at[pl.ds(0, 48)]
+        pltpu.make_async_copy(most, most, us_sem).wait()
+
     packed = add_up(gz, 0)
     gx[x * 4 + y] = packed
     for dx in FAR4:
         for dy in FAR4:
             if dx or dy:
                 share(gx, x * 4 + y, 1, device(z, rem(x + dx, NX), rem(y + dy, NY), core))
+    for b in range(CHUNKS):
+        rest = bsend.at[b, pl.ds(0, 15)]
+        pltpu.make_async_copy(rest, rest, bs_sem.at[b]).wait()
     packed = add_up(gx, 1)
+    for stage, buf in enumerate((gz, gx)):
+        some = buf.at[pl.ds(0, 15)]
+        pltpu.make_async_copy(some, some, qs_sem.at[stage]).wait()
 
     turned = [packed] + [pltpu.roll(packed, n * PS, 1) for n in range(1, 4)]
     strips = []
@@ -388,38 +419,18 @@
     answer = jnp.dot(left(inverse), right(mine), preferred_element_type=F32)
     result[...] = answer[:, :TILE] * (math.sqrt(NB * M) / jnp.sqrt(scale))
 
-    for copy in sends + gathers + swaps:
-        copy.wait_send()
-    for stage, buf in enumerate((gz, gx)):
-        some = buf.at[pl.ds(0, 15)]
-        pltpu.make_async_copy(some, some, qs_sem.at[stage]).wait()
-    for b in range(CHUNKS):
-        rest = bsend.at[b, pl.ds(0, 15)]
-        pltpu.make_async_copy(rest, rest, bs_sem.at[b]).wait()
-
-    @pl.when(my_block < BLOCKS)
-    def _():
-        most = mid.at[pl.ds(0, 47)]
-        pltpu.make_async_copy(most, most, us_sem).wait()
-        most = mid.at[pl.ds(0, 63)]
-        pltpu.make_async_copy(most, most, gs_sem).wait()
-
-    @pl.when(my_block >= BLOCKS)
-    def _():
-        most = mid.at[pl.ds(0, 48)]
-        pltpu.make_async_copy(most, most, us_sem).wait()
-
 
 def shards(damping, block_seeds):
     mix, out, back, last = tables()
-    vmem, anywhere = pl.BlockSpec(memory_space=pltpu.VMEM), pl.BlockSpec(memory_space=pl.ANY)
+    vmem, hbm = pl.BlockSpec(memory_space=pltpu.VMEM), pl.BlockSpec(memory_space=pltpu.HBM)
     dma = pltpu.SemaphoreType.DMA
     turned = pl.pallas_call(
         kernel,
         out_shape=jax.ShapeDtypeStruct((PS, TILE), F32),
-        in_specs=[pl.BlockSpec(memory_space=pltpu.SMEM)] + [anywhere] * 5,
+        in_specs=[hbm] * 6,
         out_specs=vmem,
         scratch_shapes=[
+            pltpu.SMEM((NB,), jnp.int32),
             pltpu.VMEM((TILE, OWN, M), BF16),
             pltpu.VMEM((TILE * OWN, M), BF16),
             pltpu.VMEM((KC, NB * PS), F32),
@@ -438,12 +449,12 @@
             pltpu.VMEM((CHUNKS, 16, 16, 128), BF16),
             pltpu.VMEM((16, 8, 128), F32),
             pltpu.VMEM((16, 8, 128), F32),
-            pltpu.SemaphoreType.REGULAR, dma((5,)), dma((CHUNKS, 3)), dma((CHUNKS, 3)), dma, dma, dma,
+            pltpu.SemaphoreType.REGULAR, dma((6,)), dma((CHUNKS, 3)), dma((CHUNKS, 3)), dma, dma, dma,
             dma((CHUNKS,)), dma((CHUNKS, 3)), dma((CHUNKS, 3)), dma((CHUNKS,)), dma((CHUNKS,)),
             dma((CHUNKS,)), dma((CHUNKS,)), dma((2,)), dma((2,)),
         ],
         compiler_params=pltpu.CompilerParams(
-            collective_id=0, has_side_effects=True, vmem_limit_bytes=62 << 20),
+            collective_id=0, has_side_effects=True, vmem_limit_bytes=40 << 20),
         name="hankel",
     )(block_seeds, damping, jnp.asarray(mix), jnp.asarray(out), jnp.asarray(back), jnp.asarray(last))
     return turned.T[None]

time: 62.5 us -> 67.4 us (1.078)
  local copies, waits for them, and re-layouts: 1.38 us -> 6.96 us
  Pallas kernels: 61 us -> 60.2 us
    unnamed x1 -> x13, local copies, waits for them, and re-layouts: 1.38 us -> 6.96 us
    pallas_call x1, Pallas kernels: 61 us -> 60.2 us  [shards(): pl.pallas_call(kernel, out_shape=jax.ShapeDtypeStruct((PS, TILE), F32), i...]
where the time goes in v5:
time: 67.4 us; the launch traced here: 67.1 us
  Pallas kernels  60.2 us (89%)
  local copies, waits for them, and re-layouts  6.96 us (10%)
    pallas_call x1, Pallas kernels, shards(): pl.pallas_call(kernel, out_shape=jax.ShapeDtypeStruct((PS, TILE), F32), i...  60.2 us
    unnamed x13, local copies, waits for them, and re-layouts  6.96 us

profile of v5, /device:TPU:1, one launch (start us, length us, event | category | flops | bytes accessed | tf_op | source)
XLA Modules:
  0.0 67.1 jit_solution(10794053892766021602)
XLA Ops:
  0.0 0.0 copy-start
  0.0 1.7 %copy-done = bf16[192,4,1536]{2,1,0:T(4,128)(2,1)S(1)} copy-done((bf16[192,4,1536]{2,1,0:T(4,128)(2,1)S(1)}, bf16[192,4,1536]{2,1,0:T(4,128)(2,1)}, u32[]{:S(2)}) %copy-start) | copy-done | bytes 2359320
  1.7 0.0 copy-start.1
  1.7 1.2 %copy-done.1 = f32[256,1024]{1,0:T(8,128)S(1)} copy-done((f32[256,1024]{1,0:T(8,128)S(1)}, f32[256,1024]{1,0:T(8,128)}, u32[]{:S(2)}) %copy-start.1) | copy-done | bytes 1048600
  2.9 0.0 copy-start.2
  2.9 0.9 %copy-done.2 = f32[512,128]{1,0:T(8,128)S(1)} copy-done((f32[512,128]{1,0:T(8,128)S(1)}, f32[512,128]{1,0:T(8,128)}, u32[]{:S(2)}) %copy-start.2) | copy-done | bytes 262168
  3.8 0.0 copy-start.3
  3.8 0.9 %copy-done.3 = bf16[128,1024]{1,0:T(8,128)(2,1)S(1)} copy-done((bf16[128,1024]{1,0:T(8,128)(2,1)S(1)}, bf16[128,1024]{1,0:T(8,128)(2,1)}, u32[]{:S(2)}) %copy-start.3) | copy-done | bytes 262168
  4.8 0.0 copy-start.4
  4.8 0.9 %copy-done.4 = bf16[512,128]{1,0:T(8,128)(2,1)S(1)} copy-done((bf16[512,128]{1,0:T(8,128)(2,1)S(1)}, bf16[512,128]{1,0:T(8,128)(2,1)}, u32[]{:S(2)}) %copy-start.4) | copy-done | bytes 131096
  5.7 0.0 copy-start.5
  5.7 0.7 copy-done.5
  6.4 60.2 %hankel.1 = f32[32,192]{1,0:T(8,128)S(1)} custom-call(s32[32]{0:T(128)S(1)} %copy-done.5, bf16[192,4,1536]{2,1,0:T(4,128)(2,1)S(1)} %copy-done, f32[256,1024]{1,0:T(8,128)S(1)} %copy-done.1, bf16[128,1024]{1,0:T(8,128)(2,1)S(1)} %copy-done.3, bf16[512,128]{1,0:T(8,128)(2,1)S(1)} %copy-done.4, f32[512,128]{1,0:T(8,128)S(1)} %copy-done.2), custom_call_target="tpu_custom_call" | custom-call | tf_op jit(solution)/shard_map/hankel/pallas_call | solution.py:427
  66.5 0.6 copy.8
Async XLA Ops:
  0.0 1.7 %copy-start = (bf16[192,4,1536]{2,1,0:T(4,128)(2,1)S(1)}, bf16[192,4,1536]{2,1,0:T(4,128)(2,1)}, u32[]{:S(2)}) copy-start(bf16[192,4,1536]{2,1,0:T(4,128)(2,1)} %damp_hbm.1) | copy-start | bytes 7077892
  1.7 1.2 %copy-start.1 = (f32[256,1024]{1,0:T(8,128)S(1)}, f32[256,1024]{1,0:T(8,128)}, u32[]{:S(2)}) copy-start(f32[256,1024]{1,0:T(8,128)} %constant.8.clone.mix_hbm) | copy-start | bytes 3145732
  2.9 0.9 %copy-start.2 = (f32[512,128]{1,0:T(8,128)S(1)}, f32[512,128]{1,0:T(8,128)}, u32[]{:S(2)}) copy-start(f32[512,128]{1,0:T(8,128)} %constant.11.clone.last_hbm) | copy-start | bytes 786436
  3.8 0.9 %copy-start.3 = (bf16[128,1024]{1,0:T(8,128)(2,1)S(1)}, bf16[128,1024]{1,0:T(8,128)(2,1)}, u32[]{:S(2)}) copy-start(bf16[128,1024]{1,0:T(8,128)(2,1)} %constant.9.clone.out_hbm) | copy-start | bytes 786436
  4.8 0.9 %copy-start.4 = (bf16[512,128]{1,0:T(8,128)(2,1)S(1)}, bf16[512,128]{1,0:T(8,128)(2,1)}, u32[]{:S(2)}) copy-start(bf16[512,128]{1,0:T(8,128)(2,1)} %constant.10.clone.back_hbm) | copy-start | bytes 393220
  5.7 0.7 copy-start.5

commit v6 on v4

--- a/solution.py
+++ b/solution.py
@@ -106,13 +106,13 @@
     return (rem(z, 4) * 8 + y * 2 + core, div(z, 4) * 4 + x)
 
 
-def kernel(seeds, damp_hbm, mix_hbm, out_hbm, back_hbm, last_hbm, result,
+def kernel(facts, damp_hbm, mix_hbm, out_hbm, back_hbm, last_hbm, result,
            damp, flat, mix, last, out_tab, back_tab, probes, fsend, xrecv, summed, mid, gsend, gbuf,
            hx, bsend, brecv, gz, gx,
            ready, load_sem, xs_sem, xr_sem, us_sem, ur_sem, gs_sem, gr_sem, as_sem, ar_sem,
            hs_sem, hr_sem, bs_sem, br_sem, qs_sem, qr_sem):
     z, x, y, core = place()
-    row, col = lax.axis_index("row"), lax.axis_index("col")
+    row = lax.axis_index("row")
     here = z * 8 + y * 2 + core
     my_chunk, my_pair, my_block = core * 2 + rem(z, 2), div(z, 2), rem(y + 4 - div(z, 2), NY)
 
@@ -141,16 +141,10 @@
     for load in loads:
         load.start()
 
-    column = col * TILE + lax.broadcasted_iota(jnp.int32, (1, TILE), 1)
-    pcol = lax.broadcasted_iota(jnp.int32, (PS, 1), 0)
-    pone = (pcol + 1).astype(F32)
-
-    @pl.loop(0, NB)
-    def _(j):
-        s = seeds[j]
-        inner = residue(residue(s * (column + 1)) * (column + 3)).astype(F32)
-        second = (residue(s * (pcol + 1)) * (pcol + 2)).astype(F32)
-        phase = inner * pone + second
+    pone = (lax.broadcasted_iota(jnp.int32, (PS, 1), 0) + 1).astype(F32)
+    second = jnp.transpose(facts[:, 128:])[TILE - 128 : TILE - 128 + PS]
+    for j in range(NB):
+        phase = facts[j : j + 1, :TILE] * pone + second[:, j : j + 1]
         phase = phase - jnp.floor(phase * (1.0 / PRIME) + 0.5) * PRIME
         t = phase * (1.0 / PRIME)
         u = t * t
@@ -158,7 +152,7 @@
         for n in (3, 2, 1, 0):
             poly = poly * u + SINE[n]
         sine = poly * t
-        probes[pl.ds(pl.multiple_of(j * PS, PS), PS), :] = (1.0 - 2.0 * sine * sine).astype(BF16)
+        probes[j * PS : (j + 1) * PS, :] = (1.0 - 2.0 * sine * sine).astype(BF16)
 
     loads[1].wait()
     spread = jnp.broadcast_to(mix[...][None], (PS, KC, NB * PS)).reshape(PS * KC, NB * PS)
@@ -410,6 +404,15 @@
         pltpu.make_async_copy(most, most, us_sem).wait()
 
 
+def factors(seeds, col):
+    lane = np.broadcast_to(np.arange(256, dtype=np.int32), (NB, 256))
+    first = (lane < TILE).astype(np.int32)
+    base, gap = lane - TILE * (1 - first), 1 + first
+    index = base + first * (col * TILE)
+    inner = residue(seeds[:, None] * (index + 1)) * (index + 1 + gap)
+    return jnp.where(first > 0, residue(inner), inner).astype(F32)
+
+
 def shards(damping, block_seeds):
     mix, out, back, last = tables()
     vmem, anywhere = pl.BlockSpec(memory_space=pltpu.VMEM), pl.BlockSpec(memory_space=pl.ANY)
@@ -417,7 +420,7 @@
     turned = pl.pallas_call(
         kernel,
         out_shape=jax.ShapeDtypeStruct((PS, TILE), F32),
-        in_specs=[pl.BlockSpec(memory_space=pltpu.SMEM)] + [anywhere] * 5,
+        in_specs=[vmem] + [anywhere] * 5,
         out_specs=vmem,
         scratch_shapes=[
             pltpu.VMEM((TILE, OWN, M), BF16),
@@ -443,9 +446,9 @@
             dma((CHUNKS,)), dma((CHUNKS,)), dma((2,)), dma((2,)),
         ],
         compiler_params=pltpu.CompilerParams(
-            collective_id=0, has_side_effects=True, vmem_limit_bytes=62 << 20),
+            collective_id=0, has_side_effects=True, vmem_limit_bytes=(53 << 20) + (13 << 16)),
         name="hankel",
-    )(block_seeds, damping, jnp.asarray(mix), jnp.asarray(out), jnp.asarray(back), jnp.asarray(last))
+    )(factors(block_seeds, lax.axis_index("col")), damping, jnp.asarray(mix), jnp.asarray(out), jnp.asarray(back), jnp.asarray(last))
     return turned.T[None]
 
 

time: 62.5 us -> 61.3 us (0.981)
  Pallas kernels: 61 us -> 59.6 us
  other arithmetic: 0 us -> 0.92 us
  local copies, waits for them, and re-layouts: 1.38 us -> 0.62 us
    pallas_call x1, Pallas kernels: 61 us -> 59.6 us  [shards(): pl.pallas_call(kernel, out_shape=jax.ShapeDtypeStruct((PS, TILE), F32), i...]
    convert_element_type x0 -> x1, other arithmetic: none -> 0.92 us  [factors(): return jnp.where(first > 0, residue(inner), inner).astype(F32)]
    unnamed x1, local copies, waits for them, and re-layouts: 1.38 us -> 0.62 us
where the time goes in v6:
time: 61.3 us; the launch traced here: 61.1 us
  Pallas kernels  59.6 us (97%)
  other arithmetic  0.92 us (2%)
  local copies, waits for them, and re-layouts  0.62 us (1%)
    pallas_call x1, Pallas kernels, shards(): pl.pallas_call(kernel, out_shape=jax.ShapeDtypeStruct((PS, TILE), F32), i...  59.6 us

profile of v6, /device:TPU:1, one launch (start us, length us, event | category | flops | bytes accessed | tf_op | source)
XLA Modules:
  0.0 61.1 jit_solution(13297848101515451826)
XLA Ops:
  0.0 0.9 %fusion.2.facts = f32[32,256]{1,0:T(8,128)S(1)} fusion(pred[32,256]{1,0:T(32,128)(4,1)} %constant.36.clone, s32[32,256]{1,0:T(8,128)} %constant.35.clone, s32[32,256]{1,0:T(8,128)} %constant.34.clone, s32[32,256]{1,0:T(8,128)} %constant.33.clone, s32[]{:T(128)S(6)} %mul.33, s32[32]{0:T(128)} %param.11), kind=kLoop, calls=%fused_computation.6 | loop fusion | flops 245760 | bytes 139396 | tf_op jit(solution)/shard_map/convert_element_type | solution.py:413
  0.9 59.6 %hankel.1 = f32[32,192]{1,0:T(8,128)S(1)} custom-call(f32[32,256]{1,0:T(8,128)S(1)} %fusion.2.facts, bf16[192,4,1536]{2,1,0:T(4,128)(2,1)} %damp_hbm.1, f32[256,1024]{1,0:T(8,128)} %constant.37.clone.mix_hbm, bf16[128,1024]{1,0:T(8,128)(2,1)} %constant.38.clone.out_hbm, bf16[512,128]{1,0:T(8,128)(2,1)} %constant.39.clone.back_hbm, ...), custom_call_target="tpu_custom_call" | custom-call | tf_op jit(solution)/shard_map/hankel/pallas_call | solution.py:420
  60.5 0.6 %copy.13 = f32[1,192,32]{1,2,0:T(8,128)} copy(f32[1,192,32]{1,2,0:T(8,128)S(1)} %bitcast.3) | data formatting | bytes 49152

commit v7 on v6

--- a/solution.py
+++ b/solution.py
@@ -15,6 +15,7 @@
 NB = 32
 NSTEPS = 12
 PRIME = 65521
+AWAY = 1 << 20
 OWN = 4
 KC = 2 * OWN
 ROWS = 32
@@ -405,12 +406,14 @@
 
 
 def factors(seeds, col):
-    lane = np.broadcast_to(np.arange(256, dtype=np.int32), (NB, 256))
-    first = (lane < TILE).astype(np.int32)
-    base, gap = lane - TILE * (1 - first), 1 + first
-    index = base + first * (col * TILE)
-    inner = residue(seeds[:, None] * (index + 1)) * (index + 1 + gap)
-    return jnp.where(first > 0, residue(inner), inner).astype(F32)
+    lane = np.arange(256, dtype=np.int32)
+    code = np.where(lane < TILE, lane, TILE - AWAY - lane).astype(np.int32)
+    start = col * TILE
+    index = np.broadcast_to(code, (NB, 256)) + start
+    first = index >= 0
+    index = jnp.where(first, index, start - AWAY - index)
+    inner = residue(seeds[:, None] * (index + 1)) * (index + jnp.where(first, 3, 2))
+    return jnp.where(first, residue(inner), inner).astype(F32)
 
 
 def shards(damping, block_seeds):

time: 61.3 us -> 62.6 us (1.021)
  other arithmetic: 0.92 us -> 2.13 us
    ge x0 -> x1, other arithmetic: none -> 0.68 us  [factors(): first = index >= 0]
    add x0 -> x1, other arithmetic: none -> 0.68 us  [factors(): index = np.broadcast_to(code, (NB, 256)) + start]
where the time goes in v7:
time: 62.6 us; the launch traced here: 62.4 us
  Pallas kernels  59.7 us (95%)
  other arithmetic  2.13 us (3%)
    pallas_call x1, Pallas kernels, shards(): pl.pallas_call(kernel, out_shape=jax.ShapeDtypeStruct((PS, TILE), F32), i...  59.7 us

profile of v7, /device:TPU:1, one launch (start us, length us, event | category | flops | bytes accessed | tf_op | source)
XLA Modules:
  0.0 62.4 jit_solution(16092044536967378153)
XLA Ops:
  0.0 0.7 %add_compare_fusion = pred[256]{0:T(512)(128)(4,1)S(1)} fusion(s32[256]{0:T(256)} %constant.34.clone, s32[]{:T(128)S(6)} %mul.26), kind=kLoop, calls=%fused_computation.16 | loop fusion | flops 512 | bytes 1284 | tf_op jit(solution)/shard_map/ge | solution.py:413
  0.7 0.7 %broadcast_add_fusion = (s32[256]{0:T(256)S(1)}, s32[256]{0:T(256)S(1)}, s32[256]{0:T(256)S(1)}) fusion(s32[256]{0:T(256)} %constant.34.clone, s32[]{:T(128)S(6)} %mul.26, s32[]{:T(128)S(6)} %sub.21), kind=kLoop, calls=%fused_computation.18 | loop fusion | flops 1024 | bytes 4104 | tf_op jit(solution)/shard_map/add | solution.py:412
  1.4 0.8 %fusion.8.facts = f32[32,256]{1,0:T(8,128)S(1)} fusion(s32[256]{0:T(256)S(1)} %get-tuple-element.6, s32[256]{0:T(256)S(1)} %get-tuple-element.7, s32[256]{0:T(256)S(1)} %get-tuple-element.5, s32[32]{0:T(128)} %param.8, pred[256]{0:T(512)(128)(4,1)S(1)} %add_compare_fusion), kind=kLoop, calls=%fused_computation.14 | loop fusion | flops 237568 | bytes 36224 | tf_op jit(solution)/shard_map/convert_element_type | solution.py:416
  2.1 59.7 %hankel.1 = f32[32,192]{1,0:T(8,128)S(1)} custom-call(f32[32,256]{1,0:T(8,128)S(1)} %fusion.8.facts, bf16[192,4,1536]{2,1,0:T(4,128)(2,1)} %damp_hbm.1, f32[256,1024]{1,0:T(8,128)} %constant.35.clone.mix_hbm, bf16[128,1024]{1,0:T(8,128)(2,1)} %constant.36.clone.out_hbm, bf16[512,128]{1,0:T(8,128)(2,1)} %constant.37.clone.back_hbm, ...), custom_call_target="tpu_custom_call" | custom-call | tf_op jit(solution)/shard_map/hankel/pallas_call | solution.py:423
  61.8 0.6 copy.9

commit v8 on v6

--- a/solution.py
+++ b/solution.py
@@ -339,13 +339,34 @@
         for dc in (1, 0):
             if d or dc:
                 share(gz, z * 2 + core, 0, device(rem(z + d, NZ), x, y, core if dc == 0 else 1 - core))
+    for copy in sends + gathers + swaps:
+        copy.wait_send()
+
+    @pl.when(my_block < BLOCKS)
+    def _():
+        most = mid.at[pl.ds(0, 47)]
+        pltpu.make_async_copy(most, most, us_sem).wait()
+        most = mid.at[pl.ds(0, 63)]
+        pltpu.make_async_copy(most, most, gs_sem).wait()
+
+    @pl.when(my_block >= BLOCKS)
+    def _():
+        most = mid.at[pl.ds(0, 48)]
+        pltpu.make_async_copy(most, most, us_sem).wait()
+
     packed = add_up(gz, 0)
     gx[x * 4 + y] = packed
     for dx in FAR4:
         for dy in FAR4:
             if dx or dy:
                 share(gx, x * 4 + y, 1, device(z, rem(x + dx, NX), rem(y + dy, NY), core))
+    for b in range(CHUNKS):
+        rest = bsend.at[b, pl.ds(0, 15)]
+        pltpu.make_async_copy(rest, rest, bs_sem.at[b]).wait()
     packed = add_up(gx, 1)
+    for stage, buf in enumerate((gz, gx)):
+        some = buf.at[pl.ds(0, 15)]
+        pltpu.make_async_copy(some, some, qs_sem.at[stage]).wait()
 
     turned = [packed] + [pltpu.roll(packed, n * PS, 1) for n in range(1, 4)]
     strips = []
@@ -381,27 +402,6 @@
             square = jnp.dot(left(both[:PS]), factor, preferred_element_type=F32)
     answer = jnp.dot(left(inverse), right(mine), preferred_element_type=F32)
     result[...] = answer[:, :TILE] * (math.sqrt(NB * M) / jnp.sqrt(scale))
-
-    for copy in sends + gathers + swaps:
-        copy.wait_send()
-    for stage, buf in enumerate((gz, gx)):
-        some = buf.at[pl.ds(0, 15)]
-        pltpu.make_async_copy(some, some, qs_sem.at[stage]).wait()
-    for b in range(CHUNKS):
-        rest = bsend.at[b, pl.ds(0, 15)]
-        pltpu.make_async_copy(rest, rest, bs_sem.at[b]).wait()
-
-    @pl.when(my_block < BLOCKS)
-    def _():
-        most = mid.at[pl.ds(0, 47)]
-        pltpu.make_async_copy(most, most, us_sem).wait()
-        most = mid.at[pl.ds(0, 63)]
-        pltpu.make_async_copy(most, most, gs_sem).wait()
-
-    @pl.when(my_block >= BLOCKS)
-    def _():
-        most = mid.at[pl.ds(0, 48)]
-        pltpu.make_async_copy(most, most, us_sem).wait()
 
 
 def factors(seeds, col):

time: 61.3 us -> 61.2 us (level)
  no operation moved by 1% of the time
where the time goes in v8:
time: 61.2 us; the launch traced here: 61.1 us
  Pallas kernels  59.5 us (97%)
  other arithmetic  0.92 us (2%)
  local copies, waits for them, and re-layouts  0.62 us (1%)
    pallas_call x1, Pallas kernels, shards(): pl.pallas_call(kernel, out_shape=jax.ShapeDtypeStruct((PS, TILE), F32), i...  59.5 us

profile of v8, /device:TPU:1, one launch (start us, length us, event | category | flops | bytes accessed | tf_op | source)
XLA Modules:
  0.0 61.1 jit_solution(5966714992418819542)
XLA Ops:
  0.0 0.9 %fusion.2.facts = f32[32,256]{1,0:T(8,128)S(1)} fusion(pred[32,256]{1,0:T(32,128)(4,1)} %constant.36.clone, s32[32,256]{1,0:T(8,128)} %constant.35.clone, s32[32,256]{1,0:T(8,128)} %constant.34.clone, s32[32,256]{1,0:T(8,128)} %constant.33.clone, s32[]{:T(128)S(6)} %mul.33, s32[32]{0:T(128)} %param.11), kind=kLoop, calls=%fused_computation.6 | loop fusion | flops 245760 | bytes 139396 | tf_op jit(solution)/shard_map/convert_element_type | solution.py:413
  0.9 59.5 %hankel.1 = f32[32,192]{1,0:T(8,128)S(1)} custom-call(f32[32,256]{1,0:T(8,128)S(1)} %fusion.2.facts, bf16[192,4,1536]{2,1,0:T(4,128)(2,1)} %damp_hbm.1, f32[256,1024]{1,0:T(8,128)} %constant.37.clone.mix_hbm, bf16[128,1024]{1,0:T(8,128)(2,1)} %constant.38.clone.out_hbm, bf16[512,128]{1,0:T(8,128)(2,1)} %constant.39.clone.back_hbm, ...), custom_call_target="tpu_custom_call" | custom-call | tf_op jit(solution)/shard_map/hankel/pallas_call | solution.py:420
  60.5 0.6 %copy.13 = f32[1,192,32]{1,2,0:T(8,128)} copy(f32[1,192,32]{1,2,0:T(8,128)S(1)} %bitcast.3) | data formatting | bytes 49152
